TPU v7x, 32 devices: a whole 2x2x4 slice. The times are simulated.
32 devices in a mesh: row: 4 (over y, x), col: 4 (over z), depth: 2 (over core).
Axes of the slice: x: 2, y: 2, z: 4, core: 2. Of those that a mesh axis runs over, the one named last changes fastest.
Arguments:
- tokens: bfloat16 [128, 8192], P(('row', 'depth'), 'col'), may hold values from -6 to 6
- cotangent: bfloat16 [128, 8192], P(('row', 'depth'), 'col'), may hold values from -6 to 6
- gate_weight: bfloat16 [8192, 14336], P('col', ('row', 'depth')), may hold values from -0.0625 to 0.0625
- up_weight: bfloat16 [8192, 14336], P('col', ('row', 'depth')), may hold values from -0.0625 to 0.0625
- down_weight: bfloat16 [14336, 8192], P(('row', 'depth'), 'col'), may hold values from -0.046875 to 0.046875
Outputs:
- layer_out: bfloat16 [128, 8192], P(('row', 'depth'), 'col')
- tokens_grad: bfloat16 [128, 8192], P(('row', 'depth'), 'col')
- gate_grad: bfloat16 [8192, 14336], P('col', ('row', 'depth'))
- up_grad: bfloat16 [8192, 14336], P('col', ('row', 'depth'))
- down_grad: bfloat16 [14336, 8192], P(('row', 'depth'), 'col')
All inputs are finite; a program needn't handle non-finite values.
Results may differ from a plain program's by a relative error of at most 0.0049.
Values may be sent and summed in bfloat16 or wider, within the bound.
A program may use at most 128 MiB of HBM per device.

v0:
```python
import math

import jax
import jax.numpy as jnp
from jax import lax
from jax.sharding import PartitionSpec as P


def swish_pair(gate_sum, up_sum):
    sigmoid_gate = jax.nn.sigmoid(gate_sum)
    return (gate_sum * sigmoid_gate * up_sum).astype(jnp.bfloat16)


def swish_grads(hidden_cot, gate_sum, up_sum):
    sigmoid_gate = jax.nn.sigmoid(gate_sum)
    gate_cot = hidden_cot * up_sum * sigmoid_gate * (1.0 + gate_sum * (1.0 - sigmoid_gate))
    up_cot = hidden_cot * gate_sum * sigmoid_gate
    return (gate_cot.astype(jnp.bfloat16), up_cot.astype(jnp.bfloat16))


def product(left, right):
    return jnp.dot(left, right, preferred_element_type=jnp.float32)


def contract_last(left, right):
    return jnp.einsum("ik,jk->ij", left, right, preferred_element_type=jnp.float32)


def contract_first(left, right):
    return jnp.einsum("ki,kj->ij", left, right, preferred_element_type=jnp.float32)


def shards(tokens, cotangent, gate_weight, up_weight, down_weight):
    gathered = lax.all_gather(tokens, ("row", "depth"), axis=0, tiled=True)
    total_rows = gathered.shape[0]
    grad_scale = 1.0 / math.sqrt(total_rows)
    gate_sum, up_sum = lax.psum(
        (product(gathered, gate_weight), product(gathered, up_weight)), "col"
    )
    hidden = swish_pair(gate_sum, up_sum)
    layer_out = lax.psum_scatter(
        product(hidden, down_weight), ("row", "depth"), scatter_dimension=0, tiled=True
    ).astype(jnp.bfloat16)
    cot_rows = lax.all_gather(cotangent, ("row", "depth"), axis=0, tiled=True)
    hidden_cot = lax.psum(contract_last(cot_rows, down_weight), "col")
    down_grad = (contract_first(hidden, cot_rows) * grad_scale).astype(jnp.bfloat16)
    gate_cot, up_cot = swish_grads(hidden_cot, gate_sum, up_sum)
    gate_grad = (contract_first(gathered, gate_cot) * grad_scale).astype(jnp.bfloat16)
    up_grad = (contract_first(gathered, up_cot) * grad_scale).astype(jnp.bfloat16)
    tokens_grad = lax.psum_scatter(
        contract_last(gate_cot, gate_weight) + contract_last(up_cot, up_weight),
        ("row", "depth"),
        scatter_dimension=0,
        tiled=True,
    ).astype(jnp.bfloat16)
    return (layer_out, tokens_grad, gate_grad, up_grad, down_grad)


def solution(mesh):
    in_specs = (
        P(("row", "depth"), "col"),
        P(("row", "depth"), "col"),
        P("col", ("row", "depth")),
        P("col", ("row", "depth")),
        P(("row", "depth"), "col"),
    )
    out_specs = (
        P(("row", "depth"), "col"),
        P(("row", "depth"), "col"),
        P("col", ("row", "depth")),
        P("col", ("row", "depth")),
        P(("row", "depth"), "col"),
    )
    return jax.shard_map(shards, mesh=mesh, in_specs=in_specs, out_specs=out_specs, check_vma=False)
```

profile of v0, /device:TPU:0, one launch (start us, length us, event | category | flops | bytes accessed | tf_op | source)
XLA Modules:
  0.0 239.0 jit_solution(3161314273013729683)
XLA Ops:
  7.2 0.0 all-reduce.3.cloned.1.call-start
  7.2 11.9 %all_gather.6 = bf16[128,2048]{1,0:T(8,128)(2,1)S(1)} all-gather(bf16[16,2048]{1,0:T(8,128)(2,1)} %param.5), channel_id=1, replica_groups=mesh['row'=4,'col'=4,'depth'=2] {'row','depth'}, dimensions={0}, use_global_device_ids=true | all-gather | bytes 589824 | tf_op jit(solution)/shard_map/all_gather | solution.py:34
  19.1 5.3 %fusion.3 = f32[128,1792]{1,0:T(8,128)} fusion(bf16[128,2048]{1,0:T(8,128)(2,1)S(1)} %all_gather.6, bf16[2048,1792]{1,0:T(8,128)(2,1)} %param.8), kind=kOutput, calls=%fused_computation.11 | convolution fusion | flops 939524096 | bytes 8781824 | tf_op jit(solution)/shard_map/dot_general | solution.py:22
  24.4 2.1 fusion.2
  26.5 9.5 %all_gather.7 = bf16[128,2048]{1,0:T(8,128)(2,1)S(1)} all-gather(bf16[16,2048]{1,0:T(8,128)(2,1)S(1)} %copy-done), channel_id=1, replica_groups=mesh['row'=4,'col'=4,'depth'=2] {'row','depth'}, dimensions={0}, use_global_device_ids=true | all-gather | bytes 589824 | tf_op jit(solution)/shard_map/all_gather | solution.py:44
  36.1 3.5 %fusion.5 = f32[128,1792]{1,0:T(8,128)} fusion(bf16[128,2048]{1,0:T(8,128)(2,1)S(1)} %all_gather.7, bf16[1792,2048]{1,0:T(8,128)(2,1)S(1)} %bitcast.25), kind=kOutput, calls=%fused_computation.13 | convolution fusion | flops 939524096 | bytes 8781824 | tf_op jit(solution)/shard_map/ik,jk->ij/dot_general | solution.py:26
  39.5 0.0 all-reduce.3.cloned.1.call-update
  39.6 0.0 reduce-scatter.3.cloned.1.call-start
  39.6 109.5 %all-reduce.3.cloned.1.call-done = (f32[128,1792]{1,0:T(8,128)}, f32[128,1792]{1,0:T(8,128)}, f32[128,1792]{1,0:T(8,128)}) async-done(((f32[128,1792]{1,0:T(8,128)}, f32[128,1792]{1,0:T(8,128)}, f32[128,1792]{1,0:T(8,128)}), (f32[128,1792]{1,0:T(8,128)}, f32[128,1792]{1,0:T(8,128)}, f32[128,1792]{1,0:T(8,128)})) %all-reduce.3.cloned.1.call-update) | async-done | bytes 2752528 | tf_op jit(solution)/shard_map/psum | solution.py:37
  149.1 2.2 multiply_convert_fusion.3
  151.3 5.2 %fusion.4 = f32[128,2048]{1,0:T(8,128)} fusion(bf16[128,1792]{1,0:T(8,128)(2,1)S(1)} %get-tuple-element.15, bf16[1792,2048]{1,0:T(8,128)(2,1)} %param.9), kind=kOutput, calls=%fused_computation.12 | convolution fusion | flops 939524096 | bytes 8847360 | tf_op jit(solution)/shard_map/dot_general | solution.py:22
  156.5 0.0 reduce-scatter.3.cloned.1.call-update
  156.5 0.2 reduce-scatter.5.cloned.1.call-start
  156.7 5.6 %fusion.6 = f32[128,2048]{1,0:T(8,128)S(1)} fusion(bf16[128,1792]{1,0:T(8,128)(2,1)S(1)} %get-tuple-element.14, bf16[2048,1792]{1,0:T(8,128)(2,1)} %param.7), kind=kOutput, calls=%fused_computation.14 | convolution fusion | flops 939524096 | bytes 8847360 | tf_op jit(solution)/shard_map/ik,jk->ij/dot_general | solution.py:26
  162.3 6.8 %convolution_add_fusion = f32[128,2048]{1,0:T(8,128)} fusion(f32[128,2048]{1,0:T(8,128)S(1)} %fusion.6, bf16[128,1792]{1,0:T(8,128)(2,1)S(1)} %get-tuple-element.13, bf16[2048,1792]{1,0:T(8,128)(2,1)} %param.8), kind=kOutput, calls=%fused_computation.5 | convolution fusion | flops 939786240 | bytes 9895936 | tf_op jit(solution)/shard_map/ik,jk->ij/dot_general | solution.py:26
  169.1 0.0 reduce-scatter.5.cloned.1.call-update
  169.1 5.1 %fusion = bf16[2048,1792]{0,1:T(8,128)(2,1)} fusion(bf16[128,1792]{1,0:T(8,128)(2,1)S(1)} %get-tuple-element.14, bf16[128,2048]{1,0:T(8,128)(2,1)S(1)} %all_gather.6), kind=kOutput, calls=%fused_computation.3 | convolution fusion | flops 946864128 | bytes 8323072 | tf_op jit(solution)/shard_map/ki,kj->ij/dot_general | solution.py:30
  174.2 10.0 %copy.10 = bf16[2048,1792]{1,0:T(8,128)(2,1)} copy(bf16[2048,1792]{0,1:T(8,128)(2,1)} %fusion) | data formatting | bytes 14680064
  184.2 5.1 %fusion.1 = bf16[2048,1792]{0,1:T(8,128)(2,1)} fusion(bf16[128,1792]{1,0:T(8,128)(2,1)S(1)} %get-tuple-element.13, bf16[128,2048]{1,0:T(8,128)(2,1)S(1)} %all_gather.6), kind=kOutput, calls=%fused_computation.4 | convolution fusion | flops 946864128 | bytes 8323072 | tf_op jit(solution)/shard_map/ki,kj->ij/dot_general | solution.py:30
  189.3 9.9 %copy.11 = bf16[2048,1792]{1,0:T(8,128)(2,1)} copy(bf16[2048,1792]{0,1:T(8,128)(2,1)} %fusion.1) | data formatting | bytes 14680064
  199.3 5.1 %multiply_convert_fusion = bf16[1792,2048]{1,0:T(8,128)(2,1)} fusion(bf16[128,1792]{1,0:T(8,128)(2,1)S(1)} %get-tuple-element.15, bf16[128,2048]{1,0:T(8,128)(2,1)S(1)} %all_gather.7), kind=kOutput, calls=%fused_computation | convolution fusion | flops 946864128 | bytes 8323072 | tf_op jit(solution)/shard_map/ki,kj->ij/dot_general | solution.py:30
  204.4 1.5 convert_element_type.31
  205.9 25.0 %reduce-scatter.5.cloned.1.call-done = f32[16,2048]{1,0:T(8,128)} async-done(((f32[128,2048]{1,0:T(8,128)}), f32[16,2048]{1,0:T(8,128)}) %reduce-scatter.5.cloned.1.call-update) | async-done | bytes 131088 | tf_op jit(solution)/shard_map/reduce_scatter | solution.py:50
  230.9 1.5 convert_element_type.34
  (13 shorter events, 0.0 us)
Async XLA Ops:
  7.2 141.9 %all-reduce.3.cloned.1.call-start = ((), (), s32[]{:S(2)}) async-start(), calls=%async_computation.4 | async-start | bytes 5505024 | tf_op jit(solution)/shard_map/psum | solution.py:37
  7.2 17.2 %slice-start = ((s8[7340032]{0:T(1024)(128)(4,1)}), s8[4194304]{0:T(1024)(128)(4,1)S(1)}, s32[]{:S(2)}) async-start(s8[7340032]{0:T(1024)(128)(4,1)} %bitcast.22), calls=%async_computation.5 | async-start | bytes 8388608
  19.1 5.3 %slice-start.1 = ((s8[7340032]{0:T(1024)(128)(4,1)}), s8[3145728]{0:T(1024)(128)(4,1)S(1)}, s32[]{:S(2)}) async-start(s8[7340032]{0:T(1024)(128)(4,1)} %bitcast.22), calls=%async_computation.6 | async-start | bytes 6291456
  19.1 17.0 %slice-start.2 = ((s8[7340032]{0:T(1024)(128)(4,1)}), s8[4194304]{0:T(1024)(128)(4,1)S(1)}, s32[]{:S(2)}) async-start(s8[7340032]{0:T(1024)(128)(4,1)} %bitcast.24), calls=%async_computation.7 | async-start | bytes 8388608
  24.4 2.1 copy-start
  24.4 11.7 %slice-start.3 = ((s8[7340032]{0:T(1024)(128)(4,1)}), s8[3145728]{0:T(1024)(128)(4,1)S(1)}, s32[]{:S(2)}) async-start(s8[7340032]{0:T(1024)(128)(4,1)} %bitcast.24), calls=%async_computation.8 | async-start | bytes 6291456
  39.6 164.8 %reduce-scatter.3.cloned.1.call-start = ((), (), s32[]{:S(2)}) async-start(), calls=%async_computation.2 | async-start | bytes 1179648 | tf_op jit(solution)/shard_map/reduce_scatter | solution.py:41
  156.5 74.4 %reduce-scatter.5.cloned.1.call-start = ((), (), s32[]{:S(2)}) async-start(), calls=%async_computation.3 | async-start | bytes 1179648 | tf_op jit(solution)/shard_map/reduce_scatter | solution.py:50
Sparse Core Ops, SparseCore 0:
  39.7 109.3 all-reduce.2
  156.6 35.0 reduce-scatter.2
  194.9 36.0 reduce-scatter.4
where the time goes:
time: 240 us; the launch traced here: 239 us
  waiting for transfers between devices  135 us (56%)
  matrix products  43.8 us (18%)
  blocking collectives  21.4 us (9%)
  local copies, waits for them, and re-layouts  19.9 us (8%)
  between operations  13.8 us (6%)
  other arithmetic  5.33 us (2%)
    psum x1, waiting for transfers between devices, shards(): lax.psum((product(gathered, gate_weight), product(gathered, up_weight)),...  109 us
    reduce_scatter x1, waiting for transfers between devices, shards(): lax.psum_scatter(contract_last(gate_cot, gate_weight) + contract_last(up_...  25 us
    unnamed x12, local copies, waits for them, and re-layouts  19.9 us
    dot_general x3, matrix products, contract_last(): jnp.einsum('ik,jk->ij', left, right, preferred_element_type=jnp.float32)  15.8 us
    dot_general x3, matrix products, contract_first(): jnp.einsum('ki,kj->ij', left, right, preferred_element_type=jnp.float32)  15.4 us
    dot_general x3, matrix products, product(): return jnp.dot(left, right, preferred_element_type=jnp.float32)  12.6 us
    all_gather x1, blocking collectives, shards(): gathered = lax.all_gather(tokens, ('row', 'depth'), axis=0, tiled=True)  11.9 us
    all_gather x1, blocking collectives, shards(): cot_rows = lax.all_gather(cotangent, ('row', 'depth'), axis=0, tiled=True)  9.54 us
  transfers between devices with their start and end apart: 3, of which 2 were waited for; matrix products, arithmetic and copies ran while one was open for 21% of the time, Pallas kernels for 0%

commit v1 on v0

v1 whole, which is shorter than its diff:
```python
import functools
import math

import jax
import jax.numpy as jnp
from jax import lax
from jax.experimental import pallas as pl
from jax.experimental.pallas import tpu as pltpu
from jax.sharding import PartitionSpec as P

F32 = jnp.float32
BF16 = jnp.bfloat16
MESH = pl.DeviceIdType.MESH
VMEM_BYTES = 58 * 1024 * 1024
AG_SKEW = 3


def dot_nn(left, right):
    return lax.dot_general(left, right, (((1,), (0,)), ((), ())), preferred_element_type=F32)


def dot_nt(left, right):
    return lax.dot_general(left, right, (((1,), (1,)), ((), ())), preferred_element_type=F32)


def dot_tn(left, right):
    return lax.dot_general(left, right, (((0,), (0,)), ((), ())), preferred_element_type=F32)


def layer_kernel(
    rows, cols, depths,
    tok, cot, gw, uw, dw,
    out, tgrad, tok_all, cot_all, res,
    gwv, uwv, dwv, part, sbuf, rbuf, acc, abuf, bsend, brecv, own,
    wsem, g1_send, g1_recv, g2_send, g2_recv,
    rs_send, rs_recv, ag_send, ag_recv,
    a_send, a_recv, b_send, b_recv,
):
    chunks, _, width = gwv.shape
    block = tok.shape[0]
    total = tok_all.shape[0]
    half = total // 2
    wire = sbuf.dtype
    r = lax.axis_index("row")
    z = lax.axis_index("col")
    d = lax.axis_index("depth")

    def rows_of(index):
        return pl.ds(pl.multiple_of(index * block, block), block)

    def weight_copies(c):
        span = slice(None) if chunks == 1 else pl.ds(pl.multiple_of(c * width, width), width)
        return (
            pltpu.make_async_copy(gw.at[:, span], gwv.at[c], wsem.at[0, c]),
            pltpu.make_async_copy(uw.at[:, span], uwv.at[c], wsem.at[1, c]),
            pltpu.make_async_copy(dw.at[span, :], dwv.at[c], wsem.at[2, c]),
        )

    for c in range(chunks):
        for copy in weight_copies(c):
            copy.start()

    barrier = pltpu.get_barrier_semaphore()
    for k in range(1, rows):
        pl.semaphore_signal(barrier, inc=1, device_id={"row": lax.rem(r + k, rows)}, device_id_type=MESH)
    for j in range(1, depths):
        pl.semaphore_signal(barrier, inc=1, device_id={"depth": lax.rem(d + j, depths)}, device_id_type=MESH)

    @pl.when(z > 0)
    def _():
        pl.semaphore_signal(barrier, inc=1, device_id={"col": z - 1}, device_id_type=MESH)

    @pl.when(z < cols - 1)
    def _():
        pl.semaphore_signal(barrier, inc=1, device_id={"col": z + 1}, device_id_type=MESH)

    for a, (mine, everyone) in enumerate(((tok, tok_all), (cot, cot_all))):
        everyone[rows_of(r * depths + d), :] = mine[...]
    acc[...] = jnp.zeros_like(acc)

    near = (rows - 1) + (depths - 1)

    @pl.when(jnp.logical_or(z == 0, z == cols - 1))
    def _():
        pl.semaphore_wait(barrier, near + 1)

    @pl.when(jnp.logical_and(z > 0, z < cols - 1))
    def _():
        pl.semaphore_wait(barrier, near + 2)

    pairs = ((tok, tok_all), (cot, cot_all))

    def first_hop(a, k, source_row):
        mine, everyone = pairs[a]
        return pltpu.make_async_remote_copy(
            src_ref=mine,
            dst_ref=everyone.at[rows_of(source_row * depths + d), :],
            send_sem=g1_send.at[a, k - 1],
            recv_sem=g1_recv.at[a, k - 1],
            device_id={"row": lax.rem(r + k, rows)},
            device_id_type=MESH,
        )

    def second_hop(a, k, j, source_depth):
        everyone = pairs[a][1]
        where = rows_of(lax.rem(r - k + rows, rows) * depths + source_depth)
        return pltpu.make_async_remote_copy(
            src_ref=everyone.at[where, :],
            dst_ref=everyone.at[where, :],
            send_sem=g2_send.at[a, k, j - 1],
            recv_sem=g2_recv.at[a, k, j - 1],
            device_id={"depth": lax.rem(d + j, depths)},
            device_id_type=MESH,
        )

    for k in range(1, rows):
        for a in range(2):
            first_hop(a, k, r).start()
    for k in range(rows):
        for a in range(2):
            if k:
                first_hop(a, k, lax.rem(r - k + rows, rows)).wait_recv()
            for j in range(1, depths):
                second_hop(a, k, j, d).start()
    for k in range(rows):
        for a in range(2):
            for j in range(1, depths):
                second_hop(a, k, j, lax.rem(d - j + depths, depths)).wait_recv()

    def position(way):
        return z if way == 0 else cols - 1 - z

    def token_rows(way):
        return pl.ds(half, half) if way == 0 else pl.ds(0, half)

    def sum_copy(way, c):
        target = lax.rem(z + 1, cols) if way == 0 else lax.rem(z + cols - 1, cols)
        return pltpu.make_async_remote_copy(
            src_ref=sbuf.at[way, c],
            dst_ref=rbuf.at[way, c],
            send_sem=rs_send.at[way, c],
            recv_sem=rs_recv.at[way, c],
            device_id={"col": target},
            device_id_type=MESH,
        )

    def result_copy(way, c):
        target = lax.rem(z + cols - 1, cols) if way == 0 else lax.rem(z + 1, cols)
        where = res.at[c, :, token_rows(way), :]
        return pltpu.make_async_remote_copy(
            src_ref=where,
            dst_ref=where,
            send_sem=ag_send.at[way, c],
            recv_sem=ag_recv.at[way, c],
            device_id={"col": target},
            device_id_type=MESH,
        )

    def partial_sums(c):
        for copy in weight_copies(c):
            copy.wait()
        part[c, 0] = dot_nn(tok_all[...], gwv[c])
        part[c, 1] = dot_nn(tok_all[...], uwv[c])
        part[c, 2] = dot_nt(cot_all[...], dwv[c])

    def pass_sum(way, c):
        at = position(way)
        mine = token_rows(way)

        @pl.when(at == 0)
        def _():
            sbuf[way, c] = part[c, :, mine, :].astype(wire)
            sum_copy(way, c).start()

        @pl.when(jnp.logical_and(at > 0, at < cols - 1))
        def _():
            sum_copy(way, c).wait_recv()
            sbuf[way, c] = (part[c, :, mine, :] + rbuf[way, c].astype(F32)).astype(wire)
            sum_copy(way, c).start()

        @pl.when(at == cols - 1)
        def _():
            sum_copy(way, c).wait_recv()
            gate = part[c, 0, mine, :] + rbuf[way, c, 0].astype(F32)
            up = part[c, 1, mine, :] + rbuf[way, c, 1].astype(F32)
            hidden_cot = part[c, 2, mine, :] + rbuf[way, c, 2].astype(F32)
            sig = jax.nn.sigmoid(gate)
            res[c, 0, mine, :] = (gate * sig * up).astype(BF16)
            res[c, 1, mine, :] = (hidden_cot * up * sig * (1.0 + gate * (1.0 - sig))).astype(BF16)
            res[c, 2, mine, :] = (hidden_cot * gate * sig).astype(BF16)
            result_copy(way, c).start()

    def pass_result(way, c):
        at = position(way)

        @pl.when(at < cols - 1)
        def _():
            result_copy(way, c).wait_recv()

        @pl.when(jnp.logical_and(at > 0, at < cols - 1))
        def _():
            result_copy(way, c).start()

    def add_outputs(c):
        acc[0] += dot_nn(res[c, 0], dwv[c])
        acc[1] += dot_nt(res[c, 1], gwv[c]) + dot_nt(res[c, 2], uwv[c])

    def step(s, carry):
        @pl.when(s < chunks)
        def _():
            partial_sums(s)

        @pl.when(jnp.logical_and(s >= 1, s < chunks + 1))
        def _():
            pass_sum(0, s - 1)
            pass_sum(1, s - 1)

        @pl.when(s >= 1 + AG_SKEW)
        def _():
            c = s - 1 - AG_SKEW
            pass_result(0, c)
            pass_result(1, c)
            add_outputs(c)

        return carry

    lax.fori_loop(0, chunks + 1 + AG_SKEW, step, 0)

    def depth_copy(a, row, j, target_depth):
        return pltpu.make_async_remote_copy(
            src_ref=acc.at[a, pl.ds(pl.multiple_of((row * depths + target_depth) * block, block), block), :],
            dst_ref=abuf.at[j - 1, row, a],
            send_sem=a_send.at[j - 1, row, a],
            recv_sem=a_recv.at[j - 1, row, a],
            device_id={"depth": lax.rem(d + j, depths)},
            device_id_type=MESH,
        )

    def row_copy(k):
        return pltpu.make_async_remote_copy(
            src_ref=bsend.at[k - 1],
            dst_ref=brecv.at[k - 1],
            send_sem=b_send.at[k - 1],
            recv_sem=b_recv.at[k - 1],
            device_id={"row": lax.rem(r + k, rows)},
            device_id_type=MESH,
        )

    for row in range(rows):
        for a in range(2):
            for j in range(1, depths):
                depth_copy(a, row, j, lax.rem(d + j, depths)).start()
    for row in range(rows):
        for a in range(2):
            for j in range(1, depths):
                depth_copy(a, row, j, lax.rem(d + j, depths)).wait_recv()
    for k in list(range(1, rows)) + [0]:
        row = lax.rem(r + k, rows)
        for a in range(2):
            value = acc[a, rows_of(row * depths + d), :]
            for j in range(1, depths):
                value = value + abuf[j - 1, row, a]
            if k:
                bsend[k - 1, a] = value.astype(wire)
            else:
                own[a] = value
        if k:
            row_copy(k).start()
    for k in range(1, rows):
        row_copy(k).wait_recv()
    for a, result in enumerate((out, tgrad)):
        value = own[a]
        for k in range(1, rows):
            value = value + brecv[k - 1, a].astype(F32)
        result[...] = value.astype(result.dtype)

    for k in range(1, rows):
        row_copy(k).wait_send()
        for a in range(2):
            first_hop(a, k, r).wait_send()
    for a in range(2):
        for k in range(rows):
            for j in range(1, depths):
                second_hop(a, k, j, d).wait_send()
                depth_copy(a, k, j, lax.rem(d + j, depths)).wait_send()

    def drain(c, carry):
        for way in range(2):
            at = position(way)

            @pl.when(at < cols - 1)
            def _():
                sum_copy(way, c).wait_send()

            @pl.when(at > 0)
            def _():
                result_copy(way, c).wait_send()

        return carry

    lax.fori_loop(0, chunks, drain, 0)


def grads_kernel(scale, tok_all, cot_all, res, gate_grad, up_grad, down_grad):
    gate_grad[...] = (dot_tn(tok_all[...], res[0, 1]) * scale).astype(BF16)
    up_grad[...] = (dot_tn(tok_all[...], res[0, 2]) * scale).astype(BF16)
    down_grad[...] = (dot_tn(res[0, 0], cot_all[...]) * scale).astype(BF16)


def shards(rows, cols, depths, tokens, cotangent, gate_weight, up_weight, down_weight):
    block, feats = tokens.shape
    units = gate_weight.shape[1]
    total = block * rows * depths
    half = total // 2
    width = 256 if units % 256 == 0 else units
    chunks = units // width
    wire = BF16 if cols <= 4 else F32
    vmem = pl.BlockSpec(memory_space=pltpu.VMEM)
    hbm = pl.BlockSpec(memory_space=pl.ANY)
    dma = pltpu.SemaphoreType.DMA
    out, tgrad, tok_all, cot_all, res = pl.pallas_call(
        functools.partial(layer_kernel, rows, cols, depths),
        out_shape=(
            jax.ShapeDtypeStruct((block, feats), BF16),
            jax.ShapeDtypeStruct((block, feats), BF16),
            jax.ShapeDtypeStruct((total, feats), BF16),
            jax.ShapeDtypeStruct((total, feats), BF16),
            jax.ShapeDtypeStruct((chunks, 3, total, width), BF16),
        ),
        in_specs=[vmem, vmem, hbm, hbm, hbm],
        out_specs=(vmem,) * 5,
        scratch_shapes=[
            pltpu.VMEM((chunks, feats, width), BF16),
            pltpu.VMEM((chunks, feats, width), BF16),
            pltpu.VMEM((chunks, width, feats), BF16),
            pltpu.VMEM((chunks, 3, total, width), F32),
            pltpu.VMEM((2, chunks, 3, half, width), wire),
            pltpu.VMEM((2, chunks, 3, half, width), wire),
            pltpu.VMEM((2, total, feats), F32),
            pltpu.VMEM((depths - 1, rows, 2, block, feats), F32),
            pltpu.VMEM((rows - 1, 2, block, feats), wire),
            pltpu.VMEM((rows - 1, 2, block, feats), wire),
            pltpu.VMEM((2, block, feats), F32),
            dma((3, chunks)),
            dma((2, rows - 1)),
            dma((2, rows - 1)),
            dma((2, rows, depths - 1)),
            dma((2, rows, depths - 1)),
            dma((2, chunks)),
            dma((2, chunks)),
            dma((2, chunks)),
            dma((2, chunks)),
            dma((depths - 1, rows, 2)),
            dma((depths - 1, rows, 2)),
            dma((rows - 1,)),
            dma((rows - 1,)),
        ],
        compiler_params=pltpu.CompilerParams(
            collective_id=0, has_side_effects=True, vmem_limit_bytes=VMEM_BYTES
        ),
    )(tokens, cotangent, gate_weight, up_weight, down_weight)

    whole = pl.BlockSpec((total, feats), lambda c: (0, 0))
    gate_grad, up_grad, down_grad = pl.pallas_call(
        functools.partial(grads_kernel, 1.0 / math.sqrt(total)),
        out_shape=(
            jax.ShapeDtypeStruct((feats, units), BF16),
            jax.ShapeDtypeStruct((feats, units), BF16),
            jax.ShapeDtypeStruct((units, feats), BF16),
        ),
        grid=(chunks,),
        in_specs=[whole, whole, pl.BlockSpec((1, 3, total, width), lambda c: (c, 0, 0, 0))],
        out_specs=(
            pl.BlockSpec((feats, width), lambda c: (0, c)),
            pl.BlockSpec((feats, width), lambda c: (0, c)),
            pl.BlockSpec((width, feats), lambda c: (c, 0)),
        ),
        compiler_params=pltpu.CompilerParams(vmem_limit_bytes=VMEM_BYTES),
    )(tok_all, cot_all, res)
    return (out, tgrad, gate_grad, up_grad, down_grad)


def solution(mesh):
    specs = (
        P(("row", "depth"), "col"),
        P(("row", "depth"), "col"),
        P("col", ("row", "depth")),
        P("col", ("row", "depth")),
        P(("row", "depth"), "col"),
    )
    sizes = (mesh.shape["row"], mesh.shape["col"], mesh.shape["depth"])
    return jax.shard_map(
        functools.partial(shards, *sizes), mesh=mesh, in_specs=specs, out_specs=specs, check_vma=False
    )
```

time: 240 us -> 244 us (1.017)
  Pallas kernels: 0 us -> 237 us
  waiting for transfers between devices: 135 us -> 0 us
  matrix products: 43.8 us -> 0 us
  blocking collectives: 21.4 us -> 0 us
  local copies, waits for them, and re-layouts: 19.9 us -> 2.94 us
  between operations: 13.8 us -> 0.64 us
  other arithmetic: 5.33 us -> 0 us
    pallas_call x0 -> x2, Pallas kernels: none -> 237 us  [the longest x1 227 us: shards(): pl.pallas_call(functools.partial(layer_kernel, rows, cols, depths), out_s...]
    psum x1 -> x0, waiting for transfers between devices: 109 us -> none  [shards(): lax.psum((product(gathered, gate_weight), product(gathered, up_weight)),...]
    dot_general x9 -> x0, matrix products: 43.8 us -> none  [the longest x3 15.8 us: contract_last(): jnp.einsum('ik,jk->ij', left, right, preferred_element_type=jnp.float32)]
    reduce_scatter x2 -> x0, waiting for transfers between devices: 25 us -> none  [the longest x1 25 us: shards(): lax.psum_scatter(contract_last(gate_cot, gate_weight) + contract_last(up_...]
    all_gather x2 -> x0, blocking collectives: 21.4 us -> none  [the longest x1 11.9 us: shards(): gathered = lax.all_gather(tokens, ('row', 'depth'), axis=0, tiled=True)]
    unnamed x12 -> x2, local copies, waits for them, and re-layouts: 19.9 us -> 2.94 us
    convert_element_type x3 -> x0, other arithmetic: 5.33 us -> none  [the longest x1 2.24 us: swish_grads(): return (gate_cot.astype(jnp.bfloat16), up_cot.astype(jnp.bfloat16))]
  transfers between devices with their start and end apart: 3 -> 0, of which waited for: 2 -> 0; matrix products, arithmetic and copies ran while one was open for 21% -> 0% of each run, Pallas kernels for 0% -> 0%
where the time goes in v1:
time: 244 us; the launch traced here: 241 us
  Pallas kernels  237 us (97%)
  local copies, waits for them, and re-layouts  2.94 us (1%)
    pallas_call x1, Pallas kernels, shards(): pl.pallas_call(functools.partial(layer_kernel, rows, cols, depths), out_s...  227 us
    pallas_call x1, Pallas kernels, shards(): pl.pallas_call(functools.partial(grads_kernel, 1.0 / math.sqrt(total)), o...  10.8 us

profile of v1, /device:TPU:0, one launch (start us, length us, event | category | flops | bytes accessed | tf_op | source)
XLA Modules:
  0.0 241.0 jit_solution(14184334447466973327)
XLA Ops:
  0.6 226.7 %shard_map.92 = (bf16[16,2048]{1,0:T(8,128)(2,1)}, bf16[16,2048]{1,0:T(8,128)(2,1)}, bf16[128,2048]{1,0:T(8,128)(2,1)}, bf16[128,2048]{1,0:T(8,128)(2,1)}, bf16[7,3,128,256]{3,2,1,0:T(8,128)(2,1)}) custom-call(bf16[16,2048]{1,0:T(8,128)(2,1)} %tok.1, bf16[16,2048]{1,0:T(8,128)(2,1)} %cot.1, bf16[2048,1792]{1,0:T(8,128)(2,1)} %gw.1, bf16[2048,1792]{1,0:T(8,128)(2,1)} %uw.1, ...), custom_call_target="tpu_custom_call" | custom-call | tf_op jit(solution)/shard_map/pallas_call | solution.py:321
  227.3 10.8 %shard_map.93 = (bf16[2048,1792]{1,0:T(8,128)(2,1)}, bf16[2048,1792]{1,0:T(8,128)(2,1)}, bf16[1792,2048]{1,0:T(8,128)(2,1)}) custom-call(bf16[128,2048]{1,0:T(8,128)(2,1)} %get-tuple-element.15.tok_all, bf16[128,2048]{1,0:T(8,128)(2,1)} %get-tuple-element.16.cot_all, bf16[7,3,128,256]{3,2,1,0:T(8,128)(2,1)} %get-tuple-element.17.res), custom_call_target="tpu_custom_call" | custom-call | tf_op jit(solution)/shard_map/pallas_call | solution.py:364
  238.1 1.5 copy.12
  239.6 1.5 copy.13

commit v2 on v1

--- a/solution.py
+++ b/solution.py
@@ -12,7 +12,6 @@
 BF16 = jnp.bfloat16
 MESH = pl.DeviceIdType.MESH
 VMEM_BYTES = 58 * 1024 * 1024
-AG_SKEW = 3
 
 
 def dot_nn(left, right):
@@ -30,7 +29,7 @@
 def layer_kernel(
     rows, cols, depths,
     tok, cot, gw, uw, dw,
-    out, tgrad, tok_all, cot_all, res,
+    sums, tok_all, cot_all, res,
     gwv, uwv, dwv, part, sbuf, rbuf, acc, abuf, bsend, brecv, own,
     wsem, g1_send, g1_recv, g2_send, g2_recv,
     rs_send, rs_recv, ag_send, ag_recv,
@@ -163,27 +162,35 @@
         part[c, 1] = dot_nn(tok_all[...], uwv[c])
         part[c, 2] = dot_nt(cot_all[...], dwv[c])
 
+    def pack(value):
+        return (value * jnp.abs(value)).astype(wire) if wire == BF16 else value
+
+    def unpack(value):
+        if wire != BF16:
+            return value
+        value = value.astype(F32)
+        root = jnp.sqrt(jnp.abs(value))
+        return jnp.where(value < 0, -root, root)
+
+    def first_sum(way, c):
+        sbuf[way, c] = pack(part[c, :, token_rows(way), :])
+        sum_copy(way, c).start()
+
     def pass_sum(way, c):
         at = position(way)
         mine = token_rows(way)
-
-        @pl.when(at == 0)
+        sum_copy(way, c).wait_recv()
+
+        @pl.when(at < cols - 1)
         def _():
-            sbuf[way, c] = part[c, :, mine, :].astype(wire)
-            sum_copy(way, c).start()
-
-        @pl.when(jnp.logical_and(at > 0, at < cols - 1))
-        def _():
-            sum_copy(way, c).wait_recv()
-            sbuf[way, c] = (part[c, :, mine, :] + rbuf[way, c].astype(F32)).astype(wire)
+            sbuf[way, c] = pack(part[c, :, mine, :] + unpack(rbuf[way, c]))
             sum_copy(way, c).start()
 
         @pl.when(at == cols - 1)
         def _():
-            sum_copy(way, c).wait_recv()
-            gate = part[c, 0, mine, :] + rbuf[way, c, 0].astype(F32)
-            up = part[c, 1, mine, :] + rbuf[way, c, 1].astype(F32)
-            hidden_cot = part[c, 2, mine, :] + rbuf[way, c, 2].astype(F32)
+            gate = part[c, 0, mine, :] + unpack(rbuf[way, c, 0])
+            up = part[c, 1, mine, :] + unpack(rbuf[way, c, 1])
+            hidden_cot = part[c, 2, mine, :] + unpack(rbuf[way, c, 2])
             sig = jax.nn.sigmoid(gate)
             res[c, 0, mine, :] = (gate * sig * up).astype(BF16)
             res[c, 1, mine, :] = (hidden_cot * up * sig * (1.0 + gate * (1.0 - sig))).astype(BF16)
@@ -191,13 +198,9 @@
             result_copy(way, c).start()
 
     def pass_result(way, c):
-        at = position(way)
-
-        @pl.when(at < cols - 1)
-        def _():
-            result_copy(way, c).wait_recv()
-
-        @pl.when(jnp.logical_and(at > 0, at < cols - 1))
+        result_copy(way, c).wait_recv()
+
+        @pl.when(position(way) > 0)
         def _():
             result_copy(way, c).start()
 
@@ -205,26 +208,45 @@
         acc[0] += dot_nn(res[c, 0], dwv[c])
         acc[1] += dot_nt(res[c, 1], gwv[c]) + dot_nt(res[c, 2], uwv[c])
 
+    last = cols - 1
+
+    def within(c):
+        return jnp.logical_and(c >= 0, c < chunks)
+
     def step(s, carry):
+        for way in range(2):
+            at = position(way)
+
+            @pl.when(jnp.logical_and(at > 0, within(s - at)))
+            def _():
+                pass_sum(way, s - at)
+
+        for way in range(2):
+            at = position(way)
+            c = s - last - (last - at)
+
+            @pl.when(jnp.logical_and(at < last, within(c)))
+            def _():
+                pass_result(way, c)
+
         @pl.when(s < chunks)
         def _():
             partial_sums(s)
-
-        @pl.when(jnp.logical_and(s >= 1, s < chunks + 1))
+            for way in range(2):
+
+                @pl.when(position(way) == 0)
+                def _():
+                    first_sum(way, s)
+
+        ready = s - last - jnp.maximum(z, last - z)
+
+        @pl.when(within(ready))
         def _():
-            pass_sum(0, s - 1)
-            pass_sum(1, s - 1)
-
-        @pl.when(s >= 1 + AG_SKEW)
-        def _():
-            c = s - 1 - AG_SKEW
-            pass_result(0, c)
-            pass_result(1, c)
-            add_outputs(c)
+            add_outputs(ready)
 
         return carry
 
-    lax.fori_loop(0, chunks + 1 + AG_SKEW, step, 0)
+    lax.fori_loop(0, chunks + 2 * last, step, 0)
 
     def depth_copy(a, row, j, target_depth):
         return pltpu.make_async_remote_copy(
@@ -261,18 +283,18 @@
             for j in range(1, depths):
                 value = value + abuf[j - 1, row, a]
             if k:
-                bsend[k - 1, a] = value.astype(wire)
+                bsend[k - 1, a] = value.astype(bsend.dtype)
             else:
                 own[a] = value
         if k:
             row_copy(k).start()
     for k in range(1, rows):
         row_copy(k).wait_recv()
-    for a, result in enumerate((out, tgrad)):
+    for a in range(2):
         value = own[a]
         for k in range(1, rows):
             value = value + brecv[k - 1, a].astype(F32)
-        result[...] = value.astype(result.dtype)
+        sums[a] = value.astype(sums.dtype)
 
     for k in range(1, rows):
         row_copy(k).wait_send()
@@ -301,7 +323,12 @@
     lax.fori_loop(0, chunks, drain, 0)
 
 
-def grads_kernel(scale, tok_all, cot_all, res, gate_grad, up_grad, down_grad):
+def grads_kernel(scale, sums, tok_all, cot_all, res, out, tgrad, gate_grad, up_grad, down_grad):
+    @pl.when(pl.program_id(0) == 0)
+    def _():
+        out[...] = sums[0]
+        tgrad[...] = sums[1]
+
     gate_grad[...] = (dot_tn(tok_all[...], res[0, 1]) * scale).astype(BF16)
     up_grad[...] = (dot_tn(tok_all[...], res[0, 2]) * scale).astype(BF16)
     down_grad[...] = (dot_tn(res[0, 0], cot_all[...]) * scale).astype(BF16)
@@ -314,21 +341,21 @@
     half = total // 2
     width = 256 if units % 256 == 0 else units
     chunks = units // width
+    late = BF16 if rows <= 4 else F32
     wire = BF16 if cols <= 4 else F32
     vmem = pl.BlockSpec(memory_space=pltpu.VMEM)
     hbm = pl.BlockSpec(memory_space=pl.ANY)
     dma = pltpu.SemaphoreType.DMA
-    out, tgrad, tok_all, cot_all, res = pl.pallas_call(
+    sums, tok_all, cot_all, res = pl.pallas_call(
         functools.partial(layer_kernel, rows, cols, depths),
         out_shape=(
-            jax.ShapeDtypeStruct((block, feats), BF16),
-            jax.ShapeDtypeStruct((block, feats), BF16),
+            jax.ShapeDtypeStruct((2, block, feats), BF16),
             jax.ShapeDtypeStruct((total, feats), BF16),
             jax.ShapeDtypeStruct((total, feats), BF16),
             jax.ShapeDtypeStruct((chunks, 3, total, width), BF16),
         ),
         in_specs=[vmem, vmem, hbm, hbm, hbm],
-        out_specs=(vmem,) * 5,
+        out_specs=(vmem,) * 4,
         scratch_shapes=[
             pltpu.VMEM((chunks, feats, width), BF16),
             pltpu.VMEM((chunks, feats, width), BF16),
@@ -338,8 +365,8 @@
             pltpu.VMEM((2, chunks, 3, half, width), wire),
             pltpu.VMEM((2, total, feats), F32),
             pltpu.VMEM((depths - 1, rows, 2, block, feats), F32),
-            pltpu.VMEM((rows - 1, 2, block, feats), wire),
-            pltpu.VMEM((rows - 1, 2, block, feats), wire),
+            pltpu.VMEM((rows - 1, 2, block, feats), late),
+            pltpu.VMEM((rows - 1, 2, block, feats), late),
             pltpu.VMEM((2, block, feats), F32),
             dma((3, chunks)),
             dma((2, rows - 1)),
@@ -361,23 +388,27 @@
     )(tokens, cotangent, gate_weight, up_weight, down_weight)
 
     whole = pl.BlockSpec((total, feats), lambda c: (0, 0))
-    gate_grad, up_grad, down_grad = pl.pallas_call(
+    small = pl.BlockSpec((block, feats), lambda c: (0, 0))
+    return pl.pallas_call(
         functools.partial(grads_kernel, 1.0 / math.sqrt(total)),
         out_shape=(
+            jax.ShapeDtypeStruct((block, feats), BF16),
+            jax.ShapeDtypeStruct((block, feats), BF16),
             jax.ShapeDtypeStruct((feats, units), BF16),
             jax.ShapeDtypeStruct((feats, units), BF16),
             jax.ShapeDtypeStruct((units, feats), BF16),
         ),
         grid=(chunks,),
-        in_specs=[whole, whole, pl.BlockSpec((1, 3, total, width), lambda c: (c, 0, 0, 0))],
+        in_specs=[pl.BlockSpec((2, block, feats), lambda c: (0, 0, 0)), whole, whole, pl.BlockSpec((1, 3, total, width), lambda c: (c, 0, 0, 0))],
         out_specs=(
+            small,
+            small,
             pl.BlockSpec((feats, width), lambda c: (0, c)),
             pl.BlockSpec((feats, width), lambda c: (0, c)),
             pl.BlockSpec((width, feats), lambda c: (c, 0)),
         ),
         compiler_params=pltpu.CompilerParams(vmem_limit_bytes=VMEM_BYTES),
-    )(tok_all, cot_all, res)
-    return (out, tgrad, gate_grad, up_grad, down_grad)
+    )(sums, tok_all, cot_all, res)
 
 
 def solution(mesh):

time: 244 us -> 92.1 us (0.38); the launches traced: 241 us -> 91.7 us
  Pallas kernels: 237 us -> 91.1 us
  local copies, waits for them, and re-layouts: 2.94 us -> 0 us
    pallas_call x1, Pallas kernels: 227 us -> 80.2 us  [shards(): pl.pallas_call(functools.partial(layer_kernel, rows, cols, depths), out_s...]
    unnamed x2 -> x0, local copies, waits for them, and re-layouts: 2.94 us -> none
where the time goes in v2:
time: 92.1 us; the launch traced here: 91.7 us
  Pallas kernels  91.1 us (99%)
    pallas_call x1, Pallas kernels, shards(): pl.pallas_call(functools.partial(layer_kernel, rows, cols, depths), out_s...  80.2 us
    pallas_call x1, Pallas kernels, shards(): pl.pallas_call(functools.partial(grads_kernel, 1.0 / math.sqrt(total)), o...  10.8 us

profile of v2, /device:TPU:0, one launch (start us, length us, event | category | flops | bytes accessed | tf_op | source)
XLA Modules:
  0.0 91.7 jit_solution(1958806243588415597)
XLA Ops:
  0.6 80.2 %shard_map.92 = (bf16[2,16,2048]{2,1,0:T(8,128)(2,1)}, bf16[128,2048]{1,0:T(8,128)(2,1)}, bf16[128,2048]{1,0:T(8,128)(2,1)}, bf16[7,3,128,256]{3,2,1,0:T(8,128)(2,1)}) custom-call(bf16[16,2048]{1,0:T(8,128)(2,1)} %tok.1, bf16[16,2048]{1,0:T(8,128)(2,1)} %cot.1, bf16[2048,1792]{1,0:T(8,128)(2,1)} %gw.1, bf16[2048,1792]{1,0:T(8,128)(2,1)} %uw.1, ...), custom_call_target="tpu_custom_call" | custom-call | tf_op jit(solution)/shard_map/pallas_call | solution.py:349
  80.8 10.8 %shard_map.93 = (bf16[16,2048]{1,0:T(8,128)(2,1)}, bf16[16,2048]{1,0:T(8,128)(2,1)}, bf16[2048,1792]{1,0:T(8,128)(2,1)}, bf16[2048,1792]{1,0:T(8,128)(2,1)}, bf16[1792,2048]{1,0:T(8,128)(2,1)}) custom-call(bf16[2,16,2048]{2,1,0:T(8,128)(2,1)} %get-tuple-element.9.sums, bf16[128,2048]{1,0:T(8,128)(2,1)} %get-tuple-element.10.tok_all, ...), custom_call_target="tpu_custom_call" | custom-call | tf_op jit(solution)/shard_map/pallas_call | solution.py:392

commit v3 on v2

--- a/solution.py
+++ b/solution.py
@@ -12,6 +12,7 @@
 BF16 = jnp.bfloat16
 MESH = pl.DeviceIdType.MESH
 VMEM_BYTES = 58 * 1024 * 1024
+HOP_STEPS = 2
 
 
 def dot_nn(left, right):
@@ -29,12 +30,12 @@
 def layer_kernel(
     rows, cols, depths,
     tok, cot, gw, uw, dw,
-    sums, tok_all, cot_all, res,
-    gwv, uwv, dwv, part, sbuf, rbuf, acc, abuf, bsend, brecv, own,
-    wsem, g1_send, g1_recv, g2_send, g2_recv,
-    rs_send, rs_recv, ag_send, ag_recv,
-    a_send, a_recv, b_send, b_recv,
+    *refs,
 ):
+    sums, refs = refs[:rows], refs[rows:]
+    tok_all, cot_all, res, gwv, uwv, dwv, part, sbuf, rbuf, acc, abuf, *refs = refs
+    wsem, g1_send, g1_recv, g2_send, g2_recv, *refs = refs
+    rs_send, rs_recv, ag_send, ag_recv, a_send, a_recv = refs
     chunks, _, width = gwv.shape
     block = tok.shape[0]
     total = tok_all.shape[0]
@@ -217,13 +218,13 @@
         for way in range(2):
             at = position(way)
 
-            @pl.when(jnp.logical_and(at > 0, within(s - at)))
+            @pl.when(jnp.logical_and(at > 0, within(s - HOP_STEPS * at)))
             def _():
-                pass_sum(way, s - at)
+                pass_sum(way, s - HOP_STEPS * at)
 
         for way in range(2):
             at = position(way)
-            c = s - last - (last - at)
+            c = s - HOP_STEPS * (last + last - at)
 
             @pl.when(jnp.logical_and(at < last, within(c)))
             def _():
@@ -238,7 +239,7 @@
                 def _():
                     first_sum(way, s)
 
-        ready = s - last - jnp.maximum(z, last - z)
+        ready = s - HOP_STEPS * (last + jnp.maximum(z, last - z))
 
         @pl.when(within(ready))
         def _():
@@ -246,7 +247,7 @@
 
         return carry
 
-    lax.fori_loop(0, chunks + 2 * last, step, 0)
+    lax.fori_loop(0, chunks + HOP_STEPS * 2 * last, step, 0)
 
     def depth_copy(a, row, j, target_depth):
         return pltpu.make_async_remote_copy(
@@ -258,16 +259,6 @@
             device_id_type=MESH,
         )
 
-    def row_copy(k):
-        return pltpu.make_async_remote_copy(
-            src_ref=bsend.at[k - 1],
-            dst_ref=brecv.at[k - 1],
-            send_sem=b_send.at[k - 1],
-            recv_sem=b_recv.at[k - 1],
-            device_id={"row": lax.rem(r + k, rows)},
-            device_id_type=MESH,
-        )
-
     for row in range(rows):
         for a in range(2):
             for j in range(1, depths):
@@ -276,28 +267,15 @@
         for a in range(2):
             for j in range(1, depths):
                 depth_copy(a, row, j, lax.rem(d + j, depths)).wait_recv()
-    for k in list(range(1, rows)) + [0]:
+    for k in range(rows):
         row = lax.rem(r + k, rows)
         for a in range(2):
             value = acc[a, rows_of(row * depths + d), :]
             for j in range(1, depths):
                 value = value + abuf[j - 1, row, a]
-            if k:
-                bsend[k - 1, a] = value.astype(bsend.dtype)
-            else:
-                own[a] = value
-        if k:
-            row_copy(k).start()
+            sums[k][a] = value.astype(sums[k].dtype)
+
     for k in range(1, rows):
-        row_copy(k).wait_recv()
-    for a in range(2):
-        value = own[a]
-        for k in range(1, rows):
-            value = value + brecv[k - 1, a].astype(F32)
-        sums[a] = value.astype(sums.dtype)
-
-    for k in range(1, rows):
-        row_copy(k).wait_send()
         for a in range(2):
             first_hop(a, k, r).wait_send()
     for a in range(2):
@@ -323,14 +301,13 @@
     lax.fori_loop(0, chunks, drain, 0)
 
 
-def grads_kernel(scale, sums, tok_all, cot_all, res, out, tgrad, gate_grad, up_grad, down_grad):
+def grads_kernel(scale, tok_all, cot_all, res, gate_grad, up_grad, down_grad, tok_t):
     @pl.when(pl.program_id(0) == 0)
     def _():
-        out[...] = sums[0]
-        tgrad[...] = sums[1]
-
-    gate_grad[...] = (dot_tn(tok_all[...], res[0, 1]) * scale).astype(BF16)
-    up_grad[...] = (dot_tn(tok_all[...], res[0, 2]) * scale).astype(BF16)
+        tok_t[...] = tok_all[...].T
+
+    gate_grad[...] = (dot_nn(tok_t[...], res[0, 1]) * scale).astype(BF16)
+    up_grad[...] = (dot_nn(tok_t[...], res[0, 2]) * scale).astype(BF16)
     down_grad[...] = (dot_tn(res[0, 0], cot_all[...]) * scale).astype(BF16)
 
 
@@ -346,16 +323,17 @@
     vmem = pl.BlockSpec(memory_space=pltpu.VMEM)
     hbm = pl.BlockSpec(memory_space=pl.ANY)
     dma = pltpu.SemaphoreType.DMA
-    sums, tok_all, cot_all, res = pl.pallas_call(
+    *sums, tok_all, cot_all, res = pl.pallas_call(
         functools.partial(layer_kernel, rows, cols, depths),
         out_shape=(
-            jax.ShapeDtypeStruct((2, block, feats), BF16),
+            jax.ShapeDtypeStruct((2, block, feats), F32),
+            *[jax.ShapeDtypeStruct((2, block, feats), late)] * (rows - 1),
             jax.ShapeDtypeStruct((total, feats), BF16),
             jax.ShapeDtypeStruct((total, feats), BF16),
             jax.ShapeDtypeStruct((chunks, 3, total, width), BF16),
         ),
         in_specs=[vmem, vmem, hbm, hbm, hbm],
-        out_specs=(vmem,) * 4,
+        out_specs=(vmem,) * (rows + 3),
         scratch_shapes=[
             pltpu.VMEM((chunks, feats, width), BF16),
             pltpu.VMEM((chunks, feats, width), BF16),
@@ -365,9 +343,6 @@
             pltpu.VMEM((2, chunks, 3, half, width), wire),
             pltpu.VMEM((2, total, feats), F32),
             pltpu.VMEM((depths - 1, rows, 2, block, feats), F32),
-            pltpu.VMEM((rows - 1, 2, block, feats), late),
-            pltpu.VMEM((rows - 1, 2, block, feats), late),
-            pltpu.VMEM((2, block, feats), F32),
             dma((3, chunks)),
             dma((2, rows - 1)),
             dma((2, rows - 1)),
@@ -379,36 +354,42 @@
             dma((2, chunks)),
             dma((depths - 1, rows, 2)),
             dma((depths - 1, rows, 2)),
-            dma((rows - 1,)),
-            dma((rows - 1,)),
         ],
         compiler_params=pltpu.CompilerParams(
             collective_id=0, has_side_effects=True, vmem_limit_bytes=VMEM_BYTES
         ),
     )(tokens, cotangent, gate_weight, up_weight, down_weight)
 
+    arrived = []
+    for k in range(1, rows):
+        ring = [(i, (i + k) % rows) for i in range(rows)]
+        arrived.append(lax.ppermute(sums[k], "row", ring))
+    out, tgrad = (
+        sum((part[a].astype(F32) for part in arrived), sums[0][a]).astype(BF16) for a in range(2)
+    )
+
     whole = pl.BlockSpec((total, feats), lambda c: (0, 0))
-    small = pl.BlockSpec((block, feats), lambda c: (0, 0))
-    return pl.pallas_call(
+    gate_grad, up_grad, down_grad = pl.pallas_call(
         functools.partial(grads_kernel, 1.0 / math.sqrt(total)),
         out_shape=(
-            jax.ShapeDtypeStruct((block, feats), BF16),
-            jax.ShapeDtypeStruct((block, feats), BF16),
             jax.ShapeDtypeStruct((feats, units), BF16),
             jax.ShapeDtypeStruct((feats, units), BF16),
             jax.ShapeDtypeStruct((units, feats), BF16),
         ),
         grid=(chunks,),
-        in_specs=[pl.BlockSpec((2, block, feats), lambda c: (0, 0, 0)), whole, whole, pl.BlockSpec((1, 3, total, width), lambda c: (c, 0, 0, 0))],
+        in_specs=[whole, whole, pl.BlockSpec((1, 3, total, width), lambda c: (c, 0, 0, 0))],
         out_specs=(
-            small,
-            small,
             pl.BlockSpec((feats, width), lambda c: (0, c)),
             pl.BlockSpec((feats, width), lambda c: (0, c)),
             pl.BlockSpec((width, feats), lambda c: (c, 0)),
         ),
+        scratch_shapes=[pltpu.VMEM((feats, total), BF16)],
+        cost_estimate=pl.CostEstimate(
+            flops=6 * total * feats * units, bytes_accessed=6 * feats * units, transcendentals=0
+        ),
         compiler_params=pltpu.CompilerParams(vmem_limit_bytes=VMEM_BYTES),
-    )(sums, tok_all, cot_all, res)
+    )(tok_all, cot_all, res)
+    return (out, tgrad, gate_grad, up_grad, down_grad)
 
 
 def solution(mesh):

time: 92.1 us -> 79.9 us (0.87)
  Pallas kernels: 91.1 us -> 73.8 us
  starting transfers between devices: 0 us -> 4.42 us
    pallas_call x1, Pallas kernels: 80.2 us -> 63.1 us  [shards(): pl.pallas_call(functools.partial(layer_kernel, rows, cols, depths), out_s...]
    ppermute x0 -> x3, starting transfers between devices: none -> 4.42 us  [shards(): arrived.append(lax.ppermute(sums[k], 'row', ring))]
  transfers between devices with their start and end apart: 0 -> 3, of which waited for: 0 -> 0; matrix products, arithmetic and copies ran while one was open for 0% -> 0% of each run, Pallas kernels for 0% -> 13%
where the time goes in v3:
time: 79.9 us; the launch traced here: 79.6 us
  Pallas kernels  73.8 us (92%)
  starting transfers between devices  4.42 us (6%)
    pallas_call x1, Pallas kernels, shards(): pl.pallas_call(functools.partial(layer_kernel, rows, cols, depths), out_s...  63.1 us
    pallas_call x1, Pallas kernels, shards(): pl.pallas_call(functools.partial(grads_kernel, 1.0 / math.sqrt(total)), o...  10.7 us
    ppermute x3, starting transfers between devices, shards(): arrived.append(lax.ppermute(sums[k], 'row', ring))  4.42 us
  transfers between devices with their start and end apart: 3, of which 0 were waited for; matrix products, arithmetic and copies ran while one was open for 0% of the time, Pallas kernels for 13%

profile of v3, /device:TPU:0, one launch (start us, length us, event | category | flops | bytes accessed | tf_op | source)
XLA Modules:
  0.0 79.6 jit_solution(12763359644997855771)
XLA Ops:
  0.6 63.1 %shard_map.92 = (f32[2,16,2048]{2,1,0:T(8,128)}, bf16[2,16,2048]{2,1,0:T(8,128)(2,1)}, bf16[2,16,2048]{2,1,0:T(8,128)(2,1)}, bf16[2,16,2048]{2,1,0:T(8,128)(2,1)...) custom-call(bf16[16,2048]{1,0:T(8,128)(2,1)} %tok.1, ...), custom_call_target="tpu_custom_call" | custom-call | tf_op jit(solution)/shard_map/pallas_call | solution.py:326
  63.7 0.0 copy-start
  63.7 1.3 %collective-permute-start = (bf16[2,16,2048]{2,1,0:T(8,128)(2,1)}, bf16[2,16,2048]{2,1,0:T(8,128)(2,1)S(1)}, u32[]{:S(2)}, u32[]{:S(2)}) collective-permute-start(bf16[2,16,2048]{2,1,0:T(8,128)(2,1)} %get-tuple-element.16), channel_id=1, source_target_pairs={{0,8},{8,16},{16,24},{24,0},{1,9},{9,17},{17,25},{25,1},{2,10},{10... | collective-permute-start | bytes 393224 | tf_op jit(solution)/shard_map/ppermute | solution.py:366
  65.0 1.5 %collective-permute-start.1 = (bf16[2,16,2048]{2,1,0:T(8,128)(2,1)}, bf16[2,16,2048]{2,1,0:T(8,128)(2,1)S(1)}, u32[]{:S(2)}, u32[]{:S(2)}) collective-permute-start(bf16[2,16,2048]{2,1,0:T(8,128)(2,1)} %get-tuple-element.17), channel_id=1, source_target_pairs={{0,16},{8,24},{16,0},{24,8},{1,17},{9,25},{17,1},{25,9},{2,18},{10... | collective-permute-start | bytes 393224 | tf_op jit(solution)/shard_map/ppermute | solution.py:366
  66.5 1.6 %collective-permute-start.2 = (bf16[2,16,2048]{2,1,0:T(8,128)(2,1)}, bf16[2,16,2048]{2,1,0:T(8,128)(2,1)S(1)}, u32[]{:S(2)}, u32[]{:S(2)}) collective-permute-start(bf16[2,16,2048]{2,1,0:T(8,128)(2,1)} %get-tuple-element.18), channel_id=1, source_target_pairs={{0,24},{8,0},{16,8},{24,16},{1,25},{9,1},{17,9},{25,17},{2,26},{10... | collective-permute-start | bytes 393224 | tf_op jit(solution)/shard_map/ppermute | solution.py:366
  68.1 10.7 %shard_map.93 = (bf16[2048,1792]{1,0:T(8,128)(2,1)}, bf16[2048,1792]{1,0:T(8,128)(2,1)}, bf16[1792,2048]{1,0:T(8,128)(2,1)}) custom-call(bf16[128,2048]{1,0:T(8,128)(2,1)} %get-tuple-element.19.tok_all, bf16[128,2048]{1,0:T(8,128)(2,1)} %get-tuple-element.20.cot_all, bf16[7,3,128,256]{3,2,1,0:T(8,128)(2,1)} %get-tuple-element.21.res), custom_call_target="tpu_custom_call" | custom-call | flops 2818572288 | bytes 22020096 | tf_op jit(solution)/shard_map/pallas_call | solution.py:372
  78.9 0.0 collective-permute-done
  78.9 0.0 collective-permute-done.1
  78.9 0.0 collective-permute-done.2
  78.9 0.0 copy-done
  78.9 0.7 fusion.1
Async XLA Ops:
  63.7 15.2 %copy-start = (f32[2,16,2048]{2,1,0:T(8,128)S(1)}, f32[2,16,2048]{2,1,0:T(8,128)}, u32[]{:S(2)}) copy-start(f32[2,16,2048]{2,1,0:T(8,128)} %get-tuple-element.15) | copy-start | bytes 786436
  63.7 15.2 %collective-permute-start = (bf16[2,16,2048]{2,1,0:T(8,128)(2,1)}, bf16[2,16,2048]{2,1,0:T(8,128)(2,1)S(1)}, u32[]{:S(2)}, u32[]{:S(2)}) collective-permute-start(bf16[2,16,2048]{2,1,0:T(8,128)(2,1)} %get-tuple-element.16), channel_id=1, source_target_pairs={{0,8},{8,16},{16,24},{24,0},{1,9},{9,17},{17,25},{25,1},{2,10},{10... | collective-permute-start | bytes 393224 | tf_op jit(solution)/shard_map/ppermute | solution.py:366
  65.0 13.8 %collective-permute-start.1 = (bf16[2,16,2048]{2,1,0:T(8,128)(2,1)}, bf16[2,16,2048]{2,1,0:T(8,128)(2,1)S(1)}, u32[]{:S(2)}, u32[]{:S(2)}) collective-permute-start(bf16[2,16,2048]{2,1,0:T(8,128)(2,1)} %get-tuple-element.17), channel_id=1, source_target_pairs={{0,16},{8,24},{16,0},{24,8},{1,17},{9,25},{17,1},{25,9},{2,18},{10... | collective-permute-start | bytes 393224 | tf_op jit(solution)/shard_map/ppermute | solution.py:366
  66.5 12.4 %collective-permute-start.2 = (bf16[2,16,2048]{2,1,0:T(8,128)(2,1)}, bf16[2,16,2048]{2,1,0:T(8,128)(2,1)S(1)}, u32[]{:S(2)}, u32[]{:S(2)}) collective-permute-start(bf16[2,16,2048]{2,1,0:T(8,128)(2,1)} %get-tuple-element.18), channel_id=1, source_target_pairs={{0,24},{8,0},{16,8},{24,16},{1,25},{9,1},{17,9},{25,17},{2,26},{10... | collective-permute-start | bytes 393224 | tf_op jit(solution)/shard_map/ppermute | solution.py:366

commit v4 on v3

--- a/solution.py
+++ b/solution.py
@@ -12,7 +12,8 @@
 BF16 = jnp.bfloat16
 MESH = pl.DeviceIdType.MESH
 VMEM_BYTES = 58 * 1024 * 1024
-HOP_STEPS = 2
+HOP_STEPS = 3
+PIECES = 2
 
 
 def dot_nn(left, right):
@@ -40,6 +41,8 @@
     block = tok.shape[0]
     total = tok_all.shape[0]
     half = total // 2
+    piece = half // PIECES
+    count = chunks * PIECES
     wire = sbuf.dtype
     r = lax.axis_index("row")
     z = lax.axis_index("col")
@@ -130,28 +133,31 @@
     def position(way):
         return z if way == 0 else cols - 1 - z
 
-    def token_rows(way):
-        return pl.ds(half, half) if way == 0 else pl.ds(0, half)
-
-    def sum_copy(way, c):
+    def place(way, u):
+        base = half if way == 0 else 0
+        rows_at = pl.multiple_of(base + lax.rem(u, PIECES) * piece, piece)
+        return lax.div(u, PIECES), pl.ds(rows_at, piece)
+
+    def sum_copy(way, u):
         target = lax.rem(z + 1, cols) if way == 0 else lax.rem(z + cols - 1, cols)
         return pltpu.make_async_remote_copy(
-            src_ref=sbuf.at[way, c],
-            dst_ref=rbuf.at[way, c],
-            send_sem=rs_send.at[way, c],
-            recv_sem=rs_recv.at[way, c],
+            src_ref=sbuf.at[way, u],
+            dst_ref=rbuf.at[way, u],
+            send_sem=rs_send.at[way, u],
+            recv_sem=rs_recv.at[way, u],
             device_id={"col": target},
             device_id_type=MESH,
         )
 
-    def result_copy(way, c):
+    def result_copy(way, u):
         target = lax.rem(z + cols - 1, cols) if way == 0 else lax.rem(z + 1, cols)
-        where = res.at[c, :, token_rows(way), :]
+        c, mine = place(way, u)
+        where = res.at[c, :, mine, :]
         return pltpu.make_async_remote_copy(
             src_ref=where,
             dst_ref=where,
-            send_sem=ag_send.at[way, c],
-            recv_sem=ag_recv.at[way, c],
+            send_sem=ag_send.at[way, u],
+            recv_sem=ag_recv.at[way, u],
             device_id={"col": target},
             device_id_type=MESH,
         )
@@ -173,37 +179,38 @@
         root = jnp.sqrt(jnp.abs(value))
         return jnp.where(value < 0, -root, root)
 
-    def first_sum(way, c):
-        sbuf[way, c] = pack(part[c, :, token_rows(way), :])
-        sum_copy(way, c).start()
-
-    def pass_sum(way, c):
+    def first_sum(way, u):
+        c, mine = place(way, u)
+        sbuf[way, u] = pack(part[c, :, mine, :])
+        sum_copy(way, u).start()
+
+    def pass_sum(way, u):
         at = position(way)
-        mine = token_rows(way)
-        sum_copy(way, c).wait_recv()
+        c, mine = place(way, u)
+        sum_copy(way, u).wait_recv()
 
         @pl.when(at < cols - 1)
         def _():
-            sbuf[way, c] = pack(part[c, :, mine, :] + unpack(rbuf[way, c]))
-            sum_copy(way, c).start()
+            sbuf[way, u] = pack(part[c, :, mine, :] + unpack(rbuf[way, u]))
+            sum_copy(way, u).start()
 
         @pl.when(at == cols - 1)
         def _():
-            gate = part[c, 0, mine, :] + unpack(rbuf[way, c, 0])
-            up = part[c, 1, mine, :] + unpack(rbuf[way, c, 1])
-            hidden_cot = part[c, 2, mine, :] + unpack(rbuf[way, c, 2])
+            gate = part[c, 0, mine, :] + unpack(rbuf[way, u, 0])
+            up = part[c, 1, mine, :] + unpack(rbuf[way, u, 1])
+            hidden_cot = part[c, 2, mine, :] + unpack(rbuf[way, u, 2])
             sig = jax.nn.sigmoid(gate)
             res[c, 0, mine, :] = (gate * sig * up).astype(BF16)
             res[c, 1, mine, :] = (hidden_cot * up * sig * (1.0 + gate * (1.0 - sig))).astype(BF16)
             res[c, 2, mine, :] = (hidden_cot * gate * sig).astype(BF16)
-            result_copy(way, c).start()
-
-    def pass_result(way, c):
-        result_copy(way, c).wait_recv()
+            result_copy(way, u).start()
+
+    def pass_result(way, u):
+        result_copy(way, u).wait_recv()
 
         @pl.when(position(way) > 0)
         def _():
-            result_copy(way, c).start()
+            result_copy(way, u).start()
 
     def add_outputs(c):
         acc[0] += dot_nn(res[c, 0], dwv[c])
@@ -211,43 +218,45 @@
 
     last = cols - 1
 
-    def within(c):
-        return jnp.logical_and(c >= 0, c < chunks)
+    def within(u):
+        return jnp.logical_and(u >= 0, u < count)
 
     def step(s, carry):
         for way in range(2):
             at = position(way)
-
-            @pl.when(jnp.logical_and(at > 0, within(s - HOP_STEPS * at)))
+            u = s - HOP_STEPS * at
+
+            @pl.when(jnp.logical_and(at > 0, within(u)))
             def _():
-                pass_sum(way, s - HOP_STEPS * at)
+                pass_sum(way, u)
 
         for way in range(2):
             at = position(way)
-            c = s - HOP_STEPS * (last + last - at)
-
-            @pl.when(jnp.logical_and(at < last, within(c)))
+            u = s - HOP_STEPS * (last + last - at)
+
+            @pl.when(jnp.logical_and(at < last, within(u)))
             def _():
-                pass_result(way, c)
-
-        @pl.when(s < chunks)
+                pass_result(way, u)
+
+        @pl.when(jnp.logical_and(s < count, lax.rem(s, PIECES) == 0))
         def _():
-            partial_sums(s)
+            partial_sums(lax.div(s, PIECES))
             for way in range(2):
 
                 @pl.when(position(way) == 0)
                 def _():
-                    first_sum(way, s)
+                    for h in range(PIECES):
+                        first_sum(way, s + h)
 
         ready = s - HOP_STEPS * (last + jnp.maximum(z, last - z))
 
-        @pl.when(within(ready))
+        @pl.when(jnp.logical_and(within(ready), lax.rem(ready + PIECES, PIECES) == PIECES - 1))
         def _():
-            add_outputs(ready)
+            add_outputs(lax.div(ready, PIECES))
 
         return carry
 
-    lax.fori_loop(0, chunks + HOP_STEPS * 2 * last, step, 0)
+    lax.fori_loop(0, count + HOP_STEPS * 2 * last, step, 0)
 
     def depth_copy(a, row, j, target_depth):
         return pltpu.make_async_remote_copy(
@@ -284,31 +293,40 @@
                 second_hop(a, k, j, d).wait_send()
                 depth_copy(a, k, j, lax.rem(d + j, depths)).wait_send()
 
-    def drain(c, carry):
+    def drain(u, carry):
         for way in range(2):
             at = position(way)
 
             @pl.when(at < cols - 1)
             def _():
-                sum_copy(way, c).wait_send()
+                sum_copy(way, u).wait_send()
 
             @pl.when(at > 0)
             def _():
-                result_copy(way, c).wait_send()
+                result_copy(way, u).wait_send()
 
         return carry
 
-    lax.fori_loop(0, chunks, drain, 0)
-
-
-def grads_kernel(scale, tok_all, cot_all, res, gate_grad, up_grad, down_grad, tok_t):
-    @pl.when(pl.program_id(0) == 0)
+    lax.fori_loop(0, count, drain, 0)
+
+
+def grads_kernel(scale, tok, cot_all, res, gate_grad, up_grad, down_grad, hidden_t):
+    chunks, _, _, width = res.shape
+    i = pl.program_id(0)
+
+    @pl.when(i == 0)
     def _():
-        tok_t[...] = tok_all[...].T
-
-    gate_grad[...] = (dot_nn(tok_t[...], res[0, 1]) * scale).astype(BF16)
-    up_grad[...] = (dot_nn(tok_t[...], res[0, 2]) * scale).astype(BF16)
-    down_grad[...] = (dot_tn(res[0, 0], cot_all[...]) * scale).astype(BF16)
+        for c in range(chunks):
+            hidden_t[pl.ds(c * width, width), :] = res[c, 0].T
+
+    tok_t = tok[...].T
+    for c in range(chunks):
+        span = pl.ds(c * width, width)
+        gate_grad[:, span] = (dot_nn(tok_t, res[c, 1]) * scale).astype(BF16)
+        up_grad[:, span] = (dot_nn(tok_t, res[c, 2]) * scale).astype(BF16)
+    size = down_grad.shape[0]
+    mine = hidden_t[pl.ds(pl.multiple_of(i * size, size), size), :]
+    down_grad[...] = (dot_nn(mine, cot_all[...]) * scale).astype(BF16)
 
 
 def shards(rows, cols, depths, tokens, cotangent, gate_weight, up_weight, down_weight):
@@ -318,6 +336,7 @@
     half = total // 2
     width = 256 if units % 256 == 0 else units
     chunks = units // width
+    count = chunks * PIECES
     late = BF16 if rows <= 4 else F32
     wire = BF16 if cols <= 4 else F32
     vmem = pl.BlockSpec(memory_space=pltpu.VMEM)
@@ -339,8 +358,8 @@
             pltpu.VMEM((chunks, feats, width), BF16),
             pltpu.VMEM((chunks, width, feats), BF16),
             pltpu.VMEM((chunks, 3, total, width), F32),
-            pltpu.VMEM((2, chunks, 3, half, width), wire),
-            pltpu.VMEM((2, chunks, 3, half, width), wire),
+            pltpu.VMEM((2, count, 3, half // PIECES, width), wire),
+            pltpu.VMEM((2, count, 3, half // PIECES, width), wire),
             pltpu.VMEM((2, total, feats), F32),
             pltpu.VMEM((depths - 1, rows, 2, block, feats), F32),
             dma((3, chunks)),
@@ -348,10 +367,10 @@
             dma((2, rows - 1)),
             dma((2, rows, depths - 1)),
             dma((2, rows, depths - 1)),
-            dma((2, chunks)),
-            dma((2, chunks)),
-            dma((2, chunks)),
-            dma((2, chunks)),
+            dma((2, count)),
+            dma((2, count)),
+            dma((2, count)),
+            dma((2, count)),
             dma((depths - 1, rows, 2)),
             dma((depths - 1, rows, 2)),
         ],
@@ -368,7 +387,7 @@
         sum((part[a].astype(F32) for part in arrived), sums[0][a]).astype(BF16) for a in range(2)
     )
 
-    whole = pl.BlockSpec((total, feats), lambda c: (0, 0))
+    steps = max(n for n in (8, 4, 2, 1) if feats % (128 * n) == 0 and units % (16 * n) == 0)
     gate_grad, up_grad, down_grad = pl.pallas_call(
         functools.partial(grads_kernel, 1.0 / math.sqrt(total)),
         out_shape=(
@@ -376,14 +395,18 @@
             jax.ShapeDtypeStruct((feats, units), BF16),
             jax.ShapeDtypeStruct((units, feats), BF16),
         ),
-        grid=(chunks,),
-        in_specs=[whole, whole, pl.BlockSpec((1, 3, total, width), lambda c: (c, 0, 0, 0))],
+        grid=(steps,),
+        in_specs=[
+            pl.BlockSpec((total, feats // steps), lambda i: (0, i)),
+            pl.BlockSpec((total, feats), lambda i: (0, 0)),
+            pl.BlockSpec((chunks, 3, total, width), lambda i: (0, 0, 0, 0)),
+        ],
         out_specs=(
-            pl.BlockSpec((feats, width), lambda c: (0, c)),
-            pl.BlockSpec((feats, width), lambda c: (0, c)),
-            pl.BlockSpec((width, feats), lambda c: (c, 0)),
+            pl.BlockSpec((feats // steps, units), lambda i: (i, 0)),
+            pl.BlockSpec((feats // steps, units), lambda i: (i, 0)),
+            pl.BlockSpec((units // steps, feats), lambda i: (i, 0)),
         ),
-        scratch_shapes=[pltpu.VMEM((feats, total), BF16)],
+        scratch_shapes=[pltpu.VMEM((units, total), BF16)],
         cost_estimate=pl.CostEstimate(
             flops=6 * total * feats * units, bytes_accessed=6 * feats * units, transcendentals=0
         ),

time: 79.9 us -> 79.8 us (level)
    pallas_call x1, Pallas kernels: 63.1 us -> 62 us  [shards(): pl.pallas_call(functools.partial(layer_kernel, rows, cols, depths), out_s...]
  transfers between devices with their start and end apart: 3 -> 3, of which waited for: 0 -> 0; matrix products, arithmetic and copies ran while one was open for 0% -> 0% of each run, Pallas kernels for 13% -> 14%
where the time goes in v4:
time: 79.8 us; the launch traced here: 79.5 us
  Pallas kernels  73.2 us (92%)
  starting transfers between devices  4.89 us (6%)
    pallas_call x1, Pallas kernels, shards(): pl.pallas_call(functools.partial(layer_kernel, rows, cols, depths), out_s...  62 us
    pallas_call x1, Pallas kernels, shards(): pl.pallas_call(functools.partial(grads_kernel, 1.0 / math.sqrt(total)), o...  11.2 us
    ppermute x3, starting transfers between devices, shards(): arrived.append(lax.ppermute(sums[k], 'row', ring))  4.89 us
  transfers between devices with their start and end apart: 3, of which 0 were waited for; matrix products, arithmetic and copies ran while one was open for 0% of the time, Pallas kernels for 14%

profile of v4, /device:TPU:0, one launch (start us, length us, event | category | flops | bytes accessed | tf_op | source)
XLA Modules:
  0.0 79.5 jit_solution(15197901485936936929)
XLA Ops:
  0.6 62.0 %shard_map.92 = (f32[2,16,2048]{2,1,0:T(8,128)}, bf16[2,16,2048]{2,1,0:T(8,128)(2,1)}, bf16[2,16,2048]{2,1,0:T(8,128)(2,1)}, bf16[2,16,2048]{2,1,0:T(8,128)(2,1)...) custom-call(bf16[16,2048]{1,0:T(8,128)(2,1)} %tok.1, ...), custom_call_target="tpu_custom_call" | custom-call | tf_op jit(solution)/shard_map/pallas_call | solution.py:345
  62.6 0.0 copy-start
  62.6 1.1 %collective-permute-start = (bf16[2,16,2048]{2,1,0:T(8,128)(2,1)}, bf16[2,16,2048]{2,1,0:T(8,128)(2,1)S(1)}, u32[]{:S(2)}, u32[]{:S(2)}) collective-permute-start(bf16[2,16,2048]{2,1,0:T(8,128)(2,1)} %get-tuple-element.16), channel_id=1, source_target_pairs={{0,8},{8,16},{16,24},{24,0},{1,9},{9,17},{17,25},{25,1},{2,10},{10... | collective-permute-start | bytes 393224 | tf_op jit(solution)/shard_map/ppermute | solution.py:385
  63.7 1.4 %collective-permute-start.1 = (bf16[2,16,2048]{2,1,0:T(8,128)(2,1)}, bf16[2,16,2048]{2,1,0:T(8,128)(2,1)S(1)}, u32[]{:S(2)}, u32[]{:S(2)}) collective-permute-start(bf16[2,16,2048]{2,1,0:T(8,128)(2,1)} %get-tuple-element.17), channel_id=1, source_target_pairs={{0,16},{8,24},{16,0},{24,8},{1,17},{9,25},{17,1},{25,9},{2,18},{10... | collective-permute-start | bytes 393224 | tf_op jit(solution)/shard_map/ppermute | solution.py:385
  65.2 2.4 %collective-permute-start.2 = (bf16[2,16,2048]{2,1,0:T(8,128)(2,1)}, bf16[2,16,2048]{2,1,0:T(8,128)(2,1)S(1)}, u32[]{:S(2)}, u32[]{:S(2)}) collective-permute-start(bf16[2,16,2048]{2,1,0:T(8,128)(2,1)} %get-tuple-element.18), channel_id=1, source_target_pairs={{0,24},{8,0},{16,8},{24,16},{1,25},{9,1},{17,9},{25,17},{2,26},{10... | collective-permute-start | bytes 393224 | tf_op jit(solution)/shard_map/ppermute | solution.py:385
  67.5 11.2 %shard_map.93 = (bf16[2048,1792]{1,0:T(8,128)(2,1)}, bf16[2048,1792]{1,0:T(8,128)(2,1)}, bf16[1792,2048]{1,0:T(8,128)(2,1)}) custom-call(bf16[128,2048]{1,0:T(8,128)(2,1)} %get-tuple-element.19.tok, bf16[128,2048]{1,0:T(8,128)(2,1)} %get-tuple-element.20.cot_all, bf16[7,3,128,256]{3,2,1,0:T(8,128)(2,1)} %get-tuple-element.21.res), custom_call_target="tpu_custom_call" | custom-call | flops 2818572288 | bytes 22020096 | tf_op jit(solution)/shard_map/pallas_call | solution.py:391
  78.7 0.0 collective-permute-done
  78.7 0.0 collective-permute-done.1
  78.7 0.0 collective-permute-done.2
  78.7 0.0 copy-done
  78.8 0.7 fusion.1
Async XLA Ops:
  62.6 16.1 %copy-start = (f32[2,16,2048]{2,1,0:T(8,128)S(1)}, f32[2,16,2048]{2,1,0:T(8,128)}, u32[]{:S(2)}) copy-start(f32[2,16,2048]{2,1,0:T(8,128)} %get-tuple-element.15) | copy-start | bytes 786436
  62.6 16.1 %collective-permute-start = (bf16[2,16,2048]{2,1,0:T(8,128)(2,1)}, bf16[2,16,2048]{2,1,0:T(8,128)(2,1)S(1)}, u32[]{:S(2)}, u32[]{:S(2)}) collective-permute-start(bf16[2,16,2048]{2,1,0:T(8,128)(2,1)} %get-tuple-element.16), channel_id=1, source_target_pairs={{0,8},{8,16},{16,24},{24,0},{1,9},{9,17},{17,25},{25,1},{2,10},{10... | collective-permute-start | bytes 393224 | tf_op jit(solution)/shard_map/ppermute | solution.py:385
  63.7 15.0 %collective-permute-start.1 = (bf16[2,16,2048]{2,1,0:T(8,128)(2,1)}, bf16[2,16,2048]{2,1,0:T(8,128)(2,1)S(1)}, u32[]{:S(2)}, u32[]{:S(2)}) collective-permute-start(bf16[2,16,2048]{2,1,0:T(8,128)(2,1)} %get-tuple-element.17), channel_id=1, source_target_pairs={{0,16},{8,24},{16,0},{24,8},{1,17},{9,25},{17,1},{25,9},{2,18},{10... | collective-permute-start | bytes 393224 | tf_op jit(solution)/shard_map/ppermute | solution.py:385
  65.2 13.6 %collective-permute-start.2 = (bf16[2,16,2048]{2,1,0:T(8,128)(2,1)}, bf16[2,16,2048]{2,1,0:T(8,128)(2,1)S(1)}, u32[]{:S(2)}, u32[]{:S(2)}) collective-permute-start(bf16[2,16,2048]{2,1,0:T(8,128)(2,1)} %get-tuple-element.18), channel_id=1, source_target_pairs={{0,24},{8,0},{16,8},{24,16},{1,25},{9,1},{17,9},{25,17},{2,26},{10... | collective-permute-start | bytes 393224 | tf_op jit(solution)/shard_map/ppermute | solution.py:385

commit v5 on v4

--- a/solution.py
+++ b/solution.py
@@ -11,7 +11,9 @@
 F32 = jnp.float32
 BF16 = jnp.bfloat16
 MESH = pl.DeviceIdType.MESH
-VMEM_BYTES = 58 * 1024 * 1024
+VMEM_BYTES = 42 * 1024 * 1024
+GRADS_VMEM_BYTES = 18 * 1024 * 1024
+EARLY = 3
 HOP_STEPS = 3
 PIECES = 2
 
@@ -116,19 +118,20 @@
             device_id_type=MESH,
         )
 
-    for k in range(1, rows):
-        for a in range(2):
-            first_hop(a, k, r).start()
-    for k in range(rows):
-        for a in range(2):
+    def gather(a):
+        for k in range(rows):
             if k:
                 first_hop(a, k, lax.rem(r - k + rows, rows)).wait_recv()
             for j in range(1, depths):
                 second_hop(a, k, j, d).start()
-    for k in range(rows):
-        for a in range(2):
+        for k in range(rows):
             for j in range(1, depths):
                 second_hop(a, k, j, lax.rem(d - j + depths, depths)).wait_recv()
+
+    for a in range(2):
+        for k in range(1, rows):
+            first_hop(a, k, r).start()
+    gather(0)
 
     def position(way):
         return z if way == 0 else cols - 1 - z
@@ -138,13 +141,15 @@
         rows_at = pl.multiple_of(base + lax.rem(u, PIECES) * piece, piece)
         return lax.div(u, PIECES), pl.ds(rows_at, piece)
 
-    def sum_copy(way, u):
+    spans = (pl.ds(0, 2), pl.ds(2, 1))
+
+    def sum_copy(way, u, g):
         target = lax.rem(z + 1, cols) if way == 0 else lax.rem(z + cols - 1, cols)
         return pltpu.make_async_remote_copy(
-            src_ref=sbuf.at[way, u],
-            dst_ref=rbuf.at[way, u],
-            send_sem=rs_send.at[way, u],
-            recv_sem=rs_recv.at[way, u],
+            src_ref=sbuf.at[way, u, spans[g]],
+            dst_ref=rbuf.at[way, u, spans[g]],
+            send_sem=rs_send.at[way, u, g],
+            recv_sem=rs_recv.at[way, u, g],
             device_id={"col": target},
             device_id_type=MESH,
         )
@@ -162,11 +167,14 @@
             device_id_type=MESH,
         )
 
-    def partial_sums(c):
-        for copy in weight_copies(c):
+    def gate_up_sums(c):
+        for copy in weight_copies(c)[:2]:
             copy.wait()
         part[c, 0] = dot_nn(tok_all[...], gwv[c])
         part[c, 1] = dot_nn(tok_all[...], uwv[c])
+
+    def cot_sums(c):
+        weight_copies(c)[2].wait()
         part[c, 2] = dot_nt(cot_all[...], dwv[c])
 
     def pack(value):
@@ -179,20 +187,28 @@
         root = jnp.sqrt(jnp.abs(value))
         return jnp.where(value < 0, -root, root)
 
-    def first_sum(way, u):
-        c, mine = place(way, u)
-        sbuf[way, u] = pack(part[c, :, mine, :])
-        sum_copy(way, u).start()
+    def first_sums(c, g):
+        for way in range(2):
+
+            @pl.when(position(way) == 0)
+            def _():
+                for h in range(PIECES):
+                    u = c * PIECES + h
+                    mine = place(way, u)[1]
+                    sbuf[way, u, spans[g]] = pack(part[c, spans[g], mine, :])
+                    sum_copy(way, u, g).start()
 
     def pass_sum(way, u):
         at = position(way)
         c, mine = place(way, u)
-        sum_copy(way, u).wait_recv()
+        for g in range(2):
+            sum_copy(way, u, g).wait_recv()
 
         @pl.when(at < cols - 1)
         def _():
             sbuf[way, u] = pack(part[c, :, mine, :] + unpack(rbuf[way, u]))
-            sum_copy(way, u).start()
+            for g in range(2):
+                sum_copy(way, u, g).start()
 
         @pl.when(at == cols - 1)
         def _():
@@ -212,52 +228,6 @@
         def _():
             result_copy(way, u).start()
 
-    def add_outputs(c):
-        acc[0] += dot_nn(res[c, 0], dwv[c])
-        acc[1] += dot_nt(res[c, 1], gwv[c]) + dot_nt(res[c, 2], uwv[c])
-
-    last = cols - 1
-
-    def within(u):
-        return jnp.logical_and(u >= 0, u < count)
-
-    def step(s, carry):
-        for way in range(2):
-            at = position(way)
-            u = s - HOP_STEPS * at
-
-            @pl.when(jnp.logical_and(at > 0, within(u)))
-            def _():
-                pass_sum(way, u)
-
-        for way in range(2):
-            at = position(way)
-            u = s - HOP_STEPS * (last + last - at)
-
-            @pl.when(jnp.logical_and(at < last, within(u)))
-            def _():
-                pass_result(way, u)
-
-        @pl.when(jnp.logical_and(s < count, lax.rem(s, PIECES) == 0))
-        def _():
-            partial_sums(lax.div(s, PIECES))
-            for way in range(2):
-
-                @pl.when(position(way) == 0)
-                def _():
-                    for h in range(PIECES):
-                        first_sum(way, s + h)
-
-        ready = s - HOP_STEPS * (last + jnp.maximum(z, last - z))
-
-        @pl.when(jnp.logical_and(within(ready), lax.rem(ready + PIECES, PIECES) == PIECES - 1))
-        def _():
-            add_outputs(lax.div(ready, PIECES))
-
-        return carry
-
-    lax.fori_loop(0, count + HOP_STEPS * 2 * last, step, 0)
-
     def depth_copy(a, row, j, target_depth):
         return pltpu.make_async_remote_copy(
             src_ref=acc.at[a, pl.ds(pl.multiple_of((row * depths + target_depth) * block, block), block), :],
@@ -268,10 +238,74 @@
             device_id_type=MESH,
         )
 
-    for row in range(rows):
-        for a in range(2):
+    def send_output(a):
+        for row in range(rows):
             for j in range(1, depths):
                 depth_copy(a, row, j, lax.rem(d + j, depths)).start()
+
+    def add_outputs(c):
+        acc[0] += dot_nn(res[c, 0], dwv[c])
+
+        @pl.when(c == chunks - 1)
+        def _():
+            send_output(0)
+
+        acc[1] += dot_nt(res[c, 1], gwv[c]) + dot_nt(res[c, 2], uwv[c])
+
+    last = cols - 1
+
+    def within(u):
+        return jnp.logical_and(u >= 0, u < count)
+
+    def step(s, carry):
+        for way in range(2):
+            at = position(way)
+            u = s - HOP_STEPS * at
+
+            @pl.when(jnp.logical_and(at > 0, within(u)))
+            def _():
+                pass_sum(way, u)
+
+        for way in range(2):
+            at = position(way)
+            u = s - HOP_STEPS * (last + last - at)
+
+            @pl.when(jnp.logical_and(at < last, within(u)))
+            def _():
+                pass_result(way, u)
+
+        @pl.when(jnp.logical_and(s < count, lax.rem(s, PIECES) == 0))
+        def _():
+            c = lax.div(s, PIECES)
+
+            @pl.when(c >= early)
+            def _():
+                gate_up_sums(c)
+                first_sums(c, 0)
+
+            cot_sums(c)
+            first_sums(c, 1)
+
+        ready = s - HOP_STEPS * (last + jnp.maximum(z, last - z))
+
+        @pl.when(jnp.logical_and(within(ready), lax.rem(ready + PIECES, PIECES) == PIECES - 1))
+        def _():
+            add_outputs(lax.div(ready, PIECES))
+
+        return carry
+
+    early = min(EARLY, chunks)
+
+    def head(c, carry):
+        gate_up_sums(c)
+        first_sums(c, 0)
+        return carry
+
+    lax.fori_loop(0, early, head, 0)
+    gather(1)
+    lax.fori_loop(0, count + HOP_STEPS * 2 * last, step, 0)
+
+    send_output(1)
     for row in range(rows):
         for a in range(2):
             for j in range(1, depths):
@@ -299,7 +333,8 @@
 
             @pl.when(at < cols - 1)
             def _():
-                sum_copy(way, u).wait_send()
+                for g in range(2):
+                    sum_copy(way, u, g).wait_send()
 
             @pl.when(at > 0)
             def _():
@@ -367,8 +402,8 @@
             dma((2, rows - 1)),
             dma((2, rows, depths - 1)),
             dma((2, rows, depths - 1)),
-            dma((2, count)),
-            dma((2, count)),
+            dma((2, count, 2)),
+            dma((2, count, 2)),
             dma((2, count)),
             dma((2, count)),
             dma((depths - 1, rows, 2)),
@@ -410,7 +445,7 @@
         cost_estimate=pl.CostEstimate(
             flops=6 * total * feats * units, bytes_accessed=6 * feats * units, transcendentals=0
         ),
-        compiler_params=pltpu.CompilerParams(vmem_limit_bytes=VMEM_BYTES),
+        compiler_params=pltpu.CompilerParams(vmem_limit_bytes=GRADS_VMEM_BYTES),
     )(tok_all, cot_all, res)
     return (out, tgrad, gate_grad, up_grad, down_grad)
 

time: 79.8 us -> 82.8 us (1.038)
  local copies, waits for them, and re-layouts: 0.01 us -> 4.78 us
  Pallas kernels: 73.2 us -> 72.3 us
    unnamed x2 -> x6, local copies, waits for them, and re-layouts: 0.01 us -> 4.78 us
    pallas_call x1, Pallas kernels: 11.2 us -> 10 us  [shards(): pl.pallas_call(functools.partial(grads_kernel, 1.0 / math.sqrt(total)), o...]
  transfers between devices with their start and end apart: 3 -> 3, of which waited for: 0 -> 0; matrix products, arithmetic and copies ran while one was open for 0% -> 0% of each run, Pallas kernels for 14% -> 12%
where the time goes in v5:
time: 82.8 us; the launch traced here: 82.6 us
  Pallas kernels  72.3 us (87%)
  local copies, waits for them, and re-layouts  4.78 us (6%)
  starting transfers between devices  4.16 us (5%)
    pallas_call x1, Pallas kernels, shards(): pl.pallas_call(functools.partial(layer_kernel, rows, cols, depths), out_s...  62.2 us
    pallas_call x1, Pallas kernels, shards(): pl.pallas_call(functools.partial(grads_kernel, 1.0 / math.sqrt(total)), o...  10 us
    unnamed x6, local copies, waits for them, and re-layouts  4.78 us
    ppermute x3, starting transfers between devices, shards(): arrived.append(lax.ppermute(sums[k], 'row', ring))  4.16 us
  transfers between devices with their start and end apart: 3, of which 0 were waited for; matrix products, arithmetic and copies ran while one was open for 0% of the time, Pallas kernels for 12%

profile of v5, /device:TPU:0, one launch (start us, length us, event | category | flops | bytes accessed | tf_op | source)
XLA Modules:
  0.0 82.6 jit_solution(13066467937498962067)
XLA Ops:
  0.6 0.0 copy-start
  0.6 3.1 %copy-done = bf16[2048,1792]{1,0:T(8,128)(2,1)S(1)} copy-done((bf16[2048,1792]{1,0:T(8,128)(2,1)S(1)}, bf16[2048,1792]{1,0:T(8,128)(2,1)}, u32[]{:S(2)}) %copy-start) | copy-done | bytes 7340056
  3.7 0.0 copy-start.1
  3.7 0.8 %copy-done.1 = bf16[16,2048]{1,0:T(8,128)(2,1)S(1)} copy-done((bf16[16,2048]{1,0:T(8,128)(2,1)S(1)}, bf16[16,2048]{1,0:T(8,128)(2,1)}, u32[]{:S(2)}) %copy-start.1) | copy-done | bytes 65560
  4.6 0.0 copy-start.2
  4.6 0.8 %copy-done.2 = bf16[16,2048]{1,0:T(8,128)(2,1)S(1)} copy-done((bf16[16,2048]{1,0:T(8,128)(2,1)S(1)}, bf16[16,2048]{1,0:T(8,128)(2,1)}, u32[]{:S(2)}) %copy-start.2) | copy-done | bytes 65560
  5.4 62.2 %shard_map.92 = (f32[2,16,2048]{2,1,0:T(8,128)S(1)}, bf16[2,16,2048]{2,1,0:T(8,128)(2,1)S(1)}, bf16[2,16,2048]{2,1,0:T(8,128)(2,1)S(1)}, bf16[2,16,2048]{2,1,0:T...) custom-call(bf16[16,2048]{1,0:T(8,128)(2,1)S(1)} %copy-done.1, ...), custom_call_target="tpu_custom_call" | custom-call | tf_op jit(solution)/shard_map/pallas_call | solution.py:380
  67.7 1.3 %collective-permute-start = (bf16[2,16,2048]{2,1,0:T(8,128)(2,1)S(1)}, bf16[2,16,2048]{2,1,0:T(8,128)(2,1)S(1)}, u32[]{:S(2)}, u32[]{:S(2)}) collective-permute-start(bf16[2,16,2048]{2,1,0:T(8,128)(2,1)S(1)} %get-tuple-element.16), channel_id=1, source_target_pairs={{0,8},{8,16},{16,24},{24,0},{1,9},{9,17},{17,25},{25,1},{2,10},{10... | collective-permute-start | bytes 393224 | tf_op jit(solution)/shard_map/ppermute | solution.py:420
  69.0 1.3 %collective-permute-start.1 = (bf16[2,16,2048]{2,1,0:T(8,128)(2,1)S(1)}, bf16[2,16,2048]{2,1,0:T(8,128)(2,1)S(1)}, u32[]{:S(2)}, u32[]{:S(2)}) collective-permute-start(bf16[2,16,2048]{2,1,0:T(8,128)(2,1)S(1)} %get-tuple-element.17), channel_id=1, source_target_pairs={{0,16},{8,24},{16,0},{24,8},{1,17},{9,25},{17,1},{25,9},{2,18},{10... | collective-permute-start | bytes 393224 | tf_op jit(solution)/shard_map/ppermute | solution.py:420
  70.3 1.5 %collective-permute-start.2 = (bf16[2,16,2048]{2,1,0:T(8,128)(2,1)S(1)}, bf16[2,16,2048]{2,1,0:T(8,128)(2,1)S(1)}, u32[]{:S(2)}, u32[]{:S(2)}) collective-permute-start(bf16[2,16,2048]{2,1,0:T(8,128)(2,1)S(1)} %get-tuple-element.18), channel_id=1, source_target_pairs={{0,24},{8,0},{16,8},{24,16},{1,25},{9,1},{17,9},{25,17},{2,26},{10... | collective-permute-start | bytes 393224 | tf_op jit(solution)/shard_map/ppermute | solution.py:420
  71.8 10.0 %shard_map.93 = (bf16[2048,1792]{1,0:T(8,128)(2,1)}, bf16[2048,1792]{1,0:T(8,128)(2,1)}, bf16[1792,2048]{1,0:T(8,128)(2,1)}) custom-call(bf16[128,2048]{1,0:T(8,128)(2,1)S(1)} %get-tuple-element.19.tok, bf16[128,2048]{1,0:T(8,128)(2,1)S(1)} %get-tuple-element.20.cot_all, bf16[7,3,128,256]{3,2,1,0:T(8,128)(2,1)S(1)} %get-tuple-element.21.res), custom_call_target="tpu_custom_call" | custom-call | flops 2818572288 | bytes 22020096 | tf_op jit(solution)/shard_map/pallas_call | solution.py:426
  81.9 0.0 collective-permute-done
  81.9 0.0 collective-permute-done.1
  81.9 0.0 collective-permute-done.2
  81.9 0.7 fusion.1
Async XLA Ops:
  0.6 3.1 %copy-start = (bf16[2048,1792]{1,0:T(8,128)(2,1)S(1)}, bf16[2048,1792]{1,0:T(8,128)(2,1)}, u32[]{:S(2)}) copy-start(bf16[2048,1792]{1,0:T(8,128)(2,1)} %gw.1) | copy-start | bytes 22020100
  3.7 0.8 %copy-start.1 = (bf16[16,2048]{1,0:T(8,128)(2,1)S(1)}, bf16[16,2048]{1,0:T(8,128)(2,1)}, u32[]{:S(2)}) copy-start(bf16[16,2048]{1,0:T(8,128)(2,1)} %tok.1) | copy-start | bytes 196612
  4.6 0.8 %copy-start.2 = (bf16[16,2048]{1,0:T(8,128)(2,1)S(1)}, bf16[16,2048]{1,0:T(8,128)(2,1)}, u32[]{:S(2)}) copy-start(bf16[16,2048]{1,0:T(8,128)(2,1)} %cot.1) | copy-start | bytes 196612
  67.7 14.2 %collective-permute-start = (bf16[2,16,2048]{2,1,0:T(8,128)(2,1)S(1)}, bf16[2,16,2048]{2,1,0:T(8,128)(2,1)S(1)}, u32[]{:S(2)}, u32[]{:S(2)}) collective-permute-start(bf16[2,16,2048]{2,1,0:T(8,128)(2,1)S(1)} %get-tuple-element.16), channel_id=1, source_target_pairs={{0,8},{8,16},{16,24},{24,0},{1,9},{9,17},{17,25},{25,1},{2,10},{10... | collective-permute-start | bytes 393224 | tf_op jit(solution)/shard_map/ppermute | solution.py:420
  69.0 12.9 %collective-permute-start.1 = (bf16[2,16,2048]{2,1,0:T(8,128)(2,1)S(1)}, bf16[2,16,2048]{2,1,0:T(8,128)(2,1)S(1)}, u32[]{:S(2)}, u32[]{:S(2)}) collective-permute-start(bf16[2,16,2048]{2,1,0:T(8,128)(2,1)S(1)} %get-tuple-element.17), channel_id=1, source_target_pairs={{0,16},{8,24},{16,0},{24,8},{1,17},{9,25},{17,1},{25,9},{2,18},{10... | collective-permute-start | bytes 393224 | tf_op jit(solution)/shard_map/ppermute | solution.py:420
  70.3 11.6 %collective-permute-start.2 = (bf16[2,16,2048]{2,1,0:T(8,128)(2,1)S(1)}, bf16[2,16,2048]{2,1,0:T(8,128)(2,1)S(1)}, u32[]{:S(2)}, u32[]{:S(2)}) collective-permute-start(bf16[2,16,2048]{2,1,0:T(8,128)(2,1)S(1)} %get-tuple-element.18), channel_id=1, source_target_pairs={{0,24},{8,0},{16,8},{24,16},{1,25},{9,1},{17,9},{25,17},{2,26},{10... | collective-permute-start | bytes 393224 | tf_op jit(solution)/shard_map/ppermute | solution.py:420

commit v6 on v5

--- a/solution.py
+++ b/solution.py
@@ -11,8 +11,7 @@
 F32 = jnp.float32
 BF16 = jnp.bfloat16
 MESH = pl.DeviceIdType.MESH
-VMEM_BYTES = 42 * 1024 * 1024
-GRADS_VMEM_BYTES = 18 * 1024 * 1024
+VMEM_BYTES = 58 * 1024 * 1024
 EARLY = 3
 HOP_STEPS = 3
 PIECES = 2
@@ -53,17 +52,18 @@
     def rows_of(index):
         return pl.ds(pl.multiple_of(index * block, block), block)
 
-    def weight_copies(c):
+    def weight_copy(c, i):
         span = slice(None) if chunks == 1 else pl.ds(pl.multiple_of(c * width, width), width)
-        return (
-            pltpu.make_async_copy(gw.at[:, span], gwv.at[c], wsem.at[0, c]),
-            pltpu.make_async_copy(uw.at[:, span], uwv.at[c], wsem.at[1, c]),
-            pltpu.make_async_copy(dw.at[span, :], dwv.at[c], wsem.at[2, c]),
-        )
-
-    for c in range(chunks):
-        for copy in weight_copies(c):
-            copy.start()
+        source = dw.at[span, :] if i == 2 else (gw, uw)[i].at[:, span]
+        return pltpu.make_async_copy(source, (gwv, uwv, dwv)[i].at[c], wsem.at[i, c])
+
+    def load(c):
+        for i in range(3):
+            weight_copy(c, i).start()
+
+    early = min(EARLY, chunks)
+    for c in range(early):
+        load(c)
 
     barrier = pltpu.get_barrier_semaphore()
     for k in range(1, rows):
@@ -168,13 +168,17 @@
         )
 
     def gate_up_sums(c):
-        for copy in weight_copies(c)[:2]:
-            copy.wait()
+        @pl.when(c + early < chunks)
+        def _():
+            load(c + early)
+
+        weight_copy(c, 0).wait()
+        weight_copy(c, 1).wait()
         part[c, 0] = dot_nn(tok_all[...], gwv[c])
         part[c, 1] = dot_nn(tok_all[...], uwv[c])
 
     def cot_sums(c):
-        weight_copies(c)[2].wait()
+        weight_copy(c, 2).wait()
         part[c, 2] = dot_nt(cot_all[...], dwv[c])
 
     def pack(value):
@@ -293,8 +297,6 @@
             add_outputs(lax.div(ready, PIECES))
 
         return carry
-
-    early = min(EARLY, chunks)
 
     def head(c, carry):
         gate_up_sums(c)
@@ -445,7 +447,7 @@
         cost_estimate=pl.CostEstimate(
             flops=6 * total * feats * units, bytes_accessed=6 * feats * units, transcendentals=0
         ),
-        compiler_params=pltpu.CompilerParams(vmem_limit_bytes=GRADS_VMEM_BYTES),
+        compiler_params=pltpu.CompilerParams(vmem_limit_bytes=VMEM_BYTES),
     )(tok_all, cot_all, res)
     return (out, tgrad, gate_grad, up_grad, down_grad)
 

time: 82.8 us -> 81.5 us (0.984)
  local copies, waits for them, and re-layouts: 4.78 us -> 0.01 us
  Pallas kernels: 72.3 us -> 75.2 us
    unnamed x6 -> x2, local copies, waits for them, and re-layouts: 4.78 us -> 0.01 us
    pallas_call x1, Pallas kernels: 62.2 us -> 64 us  [shards(): pl.pallas_call(functools.partial(layer_kernel, rows, cols, depths), out_s...]
    pallas_call x1, Pallas kernels: 10 us -> 11.2 us  [shards(): pl.pallas_call(functools.partial(grads_kernel, 1.0 / math.sqrt(total)), o...]
  transfers between devices with their start and end apart: 3 -> 3, of which waited for: 0 -> 0; matrix products, arithmetic and copies ran while one was open for 0% -> 0% of each run, Pallas kernels for 12% -> 14%
where the time goes in v6:
time: 81.5 us; the launch traced here: 81.1 us
  Pallas kernels  75.2 us (92%)
  starting transfers between devices  4.5 us (6%)
    pallas_call x1, Pallas kernels, shards(): pl.pallas_call(functools.partial(layer_kernel, rows, cols, depths), out_s...  64 us
    pallas_call x1, Pallas kernels, shards(): pl.pallas_call(functools.partial(grads_kernel, 1.0 / math.sqrt(total)), o...  11.2 us
    ppermute x3, starting transfers between devices, shards(): arrived.append(lax.ppermute(sums[k], 'row', ring))  4.5 us
  transfers between devices with their start and end apart: 3, of which 0 were waited for; matrix products, arithmetic and copies ran while one was open for 0% of the time, Pallas kernels for 14%

profile of v6, /device:TPU:0, one launch (start us, length us, event | category | flops | bytes accessed | tf_op | source)
XLA Modules:
  0.0 81.1 jit_solution(12760908531739488311)
XLA Ops:
  0.6 64.0 %shard_map.92 = (f32[2,16,2048]{2,1,0:T(8,128)}, bf16[2,16,2048]{2,1,0:T(8,128)(2,1)}, bf16[2,16,2048]{2,1,0:T(8,128)(2,1)}, bf16[2,16,2048]{2,1,0:T(8,128)(2,1)...) custom-call(bf16[16,2048]{1,0:T(8,128)(2,1)} %tok.1, ...), custom_call_target="tpu_custom_call" | custom-call | tf_op jit(solution)/shard_map/pallas_call | solution.py:382
  64.7 0.0 copy-start
  64.7 1.6 %collective-permute-start = (bf16[2,16,2048]{2,1,0:T(8,128)(2,1)}, bf16[2,16,2048]{2,1,0:T(8,128)(2,1)S(1)}, u32[]{:S(2)}, u32[]{:S(2)}) collective-permute-start(bf16[2,16,2048]{2,1,0:T(8,128)(2,1)} %get-tuple-element.16), channel_id=1, source_target_pairs={{0,8},{8,16},{16,24},{24,0},{1,9},{9,17},{17,25},{25,1},{2,10},{10... | collective-permute-start | bytes 393224 | tf_op jit(solution)/shard_map/ppermute | solution.py:422
  66.3 1.4 %collective-permute-start.1 = (bf16[2,16,2048]{2,1,0:T(8,128)(2,1)}, bf16[2,16,2048]{2,1,0:T(8,128)(2,1)S(1)}, u32[]{:S(2)}, u32[]{:S(2)}) collective-permute-start(bf16[2,16,2048]{2,1,0:T(8,128)(2,1)} %get-tuple-element.17), channel_id=1, source_target_pairs={{0,16},{8,24},{16,0},{24,8},{1,17},{9,25},{17,1},{25,9},{2,18},{10... | collective-permute-start | bytes 393224 | tf_op jit(solution)/shard_map/ppermute | solution.py:422
  67.7 1.5 %collective-permute-start.2 = (bf16[2,16,2048]{2,1,0:T(8,128)(2,1)}, bf16[2,16,2048]{2,1,0:T(8,128)(2,1)S(1)}, u32[]{:S(2)}, u32[]{:S(2)}) collective-permute-start(bf16[2,16,2048]{2,1,0:T(8,128)(2,1)} %get-tuple-element.18), channel_id=1, source_target_pairs={{0,24},{8,0},{16,8},{24,16},{1,25},{9,1},{17,9},{25,17},{2,26},{10... | collective-permute-start | bytes 393224 | tf_op jit(solution)/shard_map/ppermute | solution.py:422
  69.2 11.2 %shard_map.93 = (bf16[2048,1792]{1,0:T(8,128)(2,1)}, bf16[2048,1792]{1,0:T(8,128)(2,1)}, bf16[1792,2048]{1,0:T(8,128)(2,1)}) custom-call(bf16[128,2048]{1,0:T(8,128)(2,1)} %get-tuple-element.19.tok, bf16[128,2048]{1,0:T(8,128)(2,1)} %get-tuple-element.20.cot_all, bf16[7,3,128,256]{3,2,1,0:T(8,128)(2,1)} %get-tuple-element.21.res), custom_call_target="tpu_custom_call" | custom-call | flops 2818572288 | bytes 22020096 | tf_op jit(solution)/shard_map/pallas_call | solution.py:428
  80.4 0.0 collective-permute-done
  80.4 0.0 collective-permute-done.1
  80.4 0.0 collective-permute-done.2
  80.4 0.0 copy-done
  80.4 0.7 fusion.1
Async XLA Ops:
  64.7 15.7 %copy-start = (f32[2,16,2048]{2,1,0:T(8,128)S(1)}, f32[2,16,2048]{2,1,0:T(8,128)}, u32[]{:S(2)}) copy-start(f32[2,16,2048]{2,1,0:T(8,128)} %get-tuple-element.15) | copy-start | bytes 786436
  64.7 15.7 %collective-permute-start = (bf16[2,16,2048]{2,1,0:T(8,128)(2,1)}, bf16[2,16,2048]{2,1,0:T(8,128)(2,1)S(1)}, u32[]{:S(2)}, u32[]{:S(2)}) collective-permute-start(bf16[2,16,2048]{2,1,0:T(8,128)(2,1)} %get-tuple-element.16), channel_id=1, source_target_pairs={{0,8},{8,16},{16,24},{24,0},{1,9},{9,17},{17,25},{25,1},{2,10},{10... | collective-permute-start | bytes 393224 | tf_op jit(solution)/shard_map/ppermute | solution.py:422
  66.3 14.1 %collective-permute-start.1 = (bf16[2,16,2048]{2,1,0:T(8,128)(2,1)}, bf16[2,16,2048]{2,1,0:T(8,128)(2,1)S(1)}, u32[]{:S(2)}, u32[]{:S(2)}) collective-permute-start(bf16[2,16,2048]{2,1,0:T(8,128)(2,1)} %get-tuple-element.17), channel_id=1, source_target_pairs={{0,16},{8,24},{16,0},{24,8},{1,17},{9,25},{17,1},{25,9},{2,18},{10... | collective-permute-start | bytes 393224 | tf_op jit(solution)/shard_map/ppermute | solution.py:422
  67.7 12.8 %collective-permute-start.2 = (bf16[2,16,2048]{2,1,0:T(8,128)(2,1)}, bf16[2,16,2048]{2,1,0:T(8,128)(2,1)S(1)}, u32[]{:S(2)}, u32[]{:S(2)}) collective-permute-start(bf16[2,16,2048]{2,1,0:T(8,128)(2,1)} %get-tuple-element.18), channel_id=1, source_target_pairs={{0,24},{8,0},{16,8},{24,16},{1,25},{9,1},{17,9},{25,17},{2,26},{10... | collective-permute-start | bytes 393224 | tf_op jit(solution)/shard_map/ppermute | solution.py:422
